TPU v7x, 512 devices: a whole 4x8x8 slice. The times are simulated.
512 devices in a mesh: ctx: 64 (over y, z), head: 8 (over x, core).
Axes of the slice: x: 4, y: 8, z: 8, core: 2. Of those that a mesh axis runs over, the one named last changes fastest.
Arguments:
- probe_matrix: bfloat16 [32768, 4096], P('ctx', 'head'), may hold values from -6 to 6
- lookup_matrix: bfloat16 [32768, 4096], P('ctx', 'head'), may hold values from -6 to 6
- content_matrix: bfloat16 [32768, 4096], P('ctx', 'head'), may hold values from -6 to 6
- log_retention: float32 [32, 32768], P('head', 'ctx'), may hold values from -1.5 to 0
- following_observation_vector: bfloat16 [32768, 4096], P('ctx', 'head'), may hold values from -6 to 6
- rescaler_coefficients: float32 [4096], P('head'), may hold values from 0.25 to 1.75
- payoff_objective_coefficient: float32 [32768], P('ctx'), may hold values from 0.1 to 4
Outputs:
- surprise_payoff: float32 [32768], P('ctx')
- grad_queries: bfloat16 [32768, 4096], P('ctx', 'head')
- grad_keys: bfloat16 [32768, 4096], P('ctx', 'head')
- grad_values: bfloat16 [32768, 4096], P('ctx', 'head')
- scaling_derivative_mean: float32 [4096], P('head')
All inputs are finite; a program needn't handle non-finite values.
Results may differ from a plain program's by a relative error of at most 0.0095.
Values may be sent and summed in bfloat16 or wider, within the bound.
No kernel may reach another device: no remote copies, remote signals or barrier semaphores. Data moves between devices by JAX's collectives and lax.ppermute only.
A program may use at most 64 MiB of HBM per device.

v0:
```python
import jax
import jax.numpy as jnp
from jax import lax
from jax.sharding import PartitionSpec as P

HEAD_DIM = 128
HIDDEN_DIMENSION = 4096


EPS = 1e-06


def sent_to_all(shard, axis):
    devices = lax.axis_size(axis)
    return lax.all_to_all(
        jnp.broadcast_to(shard[None], (devices, *shard.shape)), axis, 0, 0, tiled=True
    )


def joined_along(parts, dim):
    lengths = list(parts.shape[1:])
    lengths[dim] *= parts.shape[0]
    return jnp.moveaxis(parts, 0, dim).reshape(lengths)


def collect(shard, axis, dim):
    parts = sent_to_all(shard, axis)
    return joined_along(parts, dim)


def of_everyone(shard, axis):
    return sent_to_all(shard, axis).sum(axis=0)


def packed_total(arrays, axis):
    vector, at, done = (jnp.concatenate([a.reshape(-1) for a in arrays]), 0, [])
    subtotal = of_everyone(vector, axis)
    for a in arrays:
        done.append(subtotal[at : at + a.size].reshape(a.shape))
        at += a.size
    return tuple(done)


def owner_prefix(all_totals, summary, backward):
    heads_here = summary.shape[0]
    entry_size = HEAD_DIM * HEAD_DIM
    entries = heads_here * entry_size
    count = lax.axis_size("ctx")
    columns = entries // count
    outgoing = summary.reshape(count, columns)
    spread = lax.all_to_all(outgoing, "ctx", split_axis=0, concat_axis=0, tiled=True)
    inclusive = jnp.cumsum(all_totals, axis=0).T
    exclusive = inclusive - all_totals.T
    order = lax.iota(jnp.int32, count)
    if backward:
        mask = order[None, :] > order[:, None]
        exponent = exclusive[:, None, :] - inclusive[:, :, None]
    else:
        mask = order[None, :] < order[:, None]
        exponent = exclusive[:, :, None] - inclusive[:, None, :]
    weights = jnp.where(mask[None], jnp.exp(jnp.where(mask[None], exponent, 0.0)), 0.0)
    mixed = jnp.einsum("hbc,cf->hbf", weights, spread, precision=lax.Precision.HIGHEST)
    start = lax.axis_index("ctx") * columns
    owner = (start + lax.iota(jnp.int32, columns)) // entry_size
    pick = (owner[None, :] == lax.iota(jnp.int32, heads_here)[:, None]).astype(jnp.float32)
    combined = jnp.sum(mixed * pick[:, None, :], axis=0).astype(jnp.bfloat16)
    returned = lax.all_to_all(combined, "ctx", split_axis=0, concat_axis=0, tiled=True)
    return returned.reshape(heads_here, HEAD_DIM, HEAD_DIM)


def local(
    probe_matrix,
    lookup_matrix,
    content_matrix,
    log_retention,
    following_observation_vector,
    rescaler_coefficients,
    payoff_objective_coefficient,
):
    token_rows = probe_matrix.shape[0]
    local_width = probe_matrix.shape[1]
    heads_here = local_width // HEAD_DIM
    tokens_all = token_rows * lax.axis_size("ctx")
    attn_scale = HEAD_DIM ** (-0.5)
    query_heads = probe_matrix.reshape(token_rows, heads_here, HEAD_DIM)
    key_heads = lookup_matrix.reshape(token_rows, heads_here, HEAD_DIM)
    value_heads = content_matrix.reshape(token_rows, heads_here, HEAD_DIM)
    cumulative = jnp.cumsum(log_retention, axis=1)
    token_position = lax.iota(jnp.int32, token_rows)
    causal = (token_position[:, None] >= token_position[None, :])[None]
    gaps = cumulative[:, :, None] - cumulative[:, None, :]
    decays = jnp.where(causal, jnp.exp(jnp.where(causal, gaps, 0.0)), 0.0)
    block_total = cumulative[:, -1]
    start_decay = jnp.exp(cumulative).T
    tail_decay = jnp.exp(block_total[:, None] - cumulative).T
    key_decayed = (key_heads * tail_decay[:, :, None]).astype(jnp.bfloat16)
    summary = jnp.einsum(
        "shd,she->hde", key_decayed, value_heads, preferred_element_type=jnp.float32
    )
    all_totals = collect(block_total.reshape(1, heads_here), "ctx", 0)
    state_in = owner_prefix(all_totals, summary, False)
    scores = jnp.einsum("thd,shd->hts", query_heads, key_heads, preferred_element_type=jnp.float32)
    attn_probs = (scores * attn_scale * decays).astype(jnp.bfloat16)
    local_part = jnp.einsum(
        "hts,shd->thd", attn_probs, value_heads, preferred_element_type=jnp.float32
    )
    carried = jnp.einsum("thd,hde->the", query_heads, state_in, preferred_element_type=jnp.float32)
    attn_out = local_part + attn_scale * start_decay[:, :, None] * carried
    output_flat = attn_out.reshape(token_rows, local_width)
    gained = rescaler_coefficients[None, :] * output_flat
    square, gain_square, cross_sum, target_square = packed_total(
        (
            jnp.sum(output_flat * output_flat, axis=1),
            jnp.sum(gained * gained, axis=1),
            jnp.sum(following_observation_vector * gained, axis=1),
            jnp.sum(
                following_observation_vector.astype(jnp.float32) * following_observation_vector,
                axis=1,
            ),
        ),
        "head",
    )
    rms = jnp.sqrt(square / HIDDEN_DIMENSION + EPS)
    rescaled_activations = output_flat / rms[:, None]
    predicted_minus_actual = (
        rescaler_coefficients[None, :] * rescaled_activations - following_observation_vector
    )
    discrepancy_adjoint = payoff_objective_coefficient[:, None] * predicted_minus_actual
    normalized_adjoint = discrepancy_adjoint * rescaler_coefficients[None, :]
    pred_square = gain_square / (rms * rms)
    pred_cross = cross_sum / rms
    novelty_output = (pred_square - 2.0 * pred_cross + target_square) / HIDDEN_DIMENSION
    inner_accumulation = payoff_objective_coefficient * (pred_square - pred_cross)
    grad_out = (
        (
            normalized_adjoint
            - rescaled_activations * (inner_accumulation / HIDDEN_DIMENSION)[:, None]
        )
        / rms[:, None]
    ).astype(jnp.bfloat16)
    grad_heads = grad_out.reshape(token_rows, heads_here, HEAD_DIM)
    scaling_derivative_mean = of_everyone(
        jnp.sum(discrepancy_adjoint * rescaled_activations, axis=0) / tokens_all, "ctx"
    )
    query_decayed = (query_heads * (attn_scale * start_decay)[:, :, None]).astype(jnp.bfloat16)
    back_summary = jnp.einsum(
        "thd,the->hde", query_decayed, grad_heads, preferred_element_type=jnp.float32
    )
    state_out = owner_prefix(all_totals, back_summary, True)
    grad_scores = jnp.einsum(
        "the,she->hts", grad_heads, value_heads, preferred_element_type=jnp.float32
    )
    grad_probs = (grad_scores * attn_scale * decays).astype(jnp.bfloat16)
    probe_derivative = jnp.einsum(
        "hts,shd->thd", grad_probs, key_heads, preferred_element_type=jnp.float32
    ) + attn_scale * start_decay[:, :, None] * jnp.einsum(
        "the,hde->thd", grad_heads, state_in, preferred_element_type=jnp.float32
    )
    lookup_derivative = jnp.einsum(
        "hts,thd->shd", grad_probs, query_heads, preferred_element_type=jnp.float32
    ) + tail_decay[:, :, None] * jnp.einsum(
        "she,hde->shd", value_heads, state_out, preferred_element_type=jnp.float32
    )
    content_derivative = jnp.einsum(
        "hts,the->she", attn_probs, grad_heads, preferred_element_type=jnp.float32
    ) + tail_decay[:, :, None] * jnp.einsum(
        "shd,hde->she", key_heads, state_out, preferred_element_type=jnp.float32
    )
    return (
        novelty_output,
        probe_derivative.reshape(token_rows, local_width).astype(jnp.bfloat16),
        lookup_derivative.reshape(token_rows, local_width).astype(jnp.bfloat16),
        content_derivative.reshape(token_rows, local_width).astype(jnp.bfloat16),
        scaling_derivative_mean,
    )


def solution(mesh):
    placed = (
        P("ctx", "head"),
        P("ctx", "head"),
        P("ctx", "head"),
        P("head", "ctx"),
        P("ctx", "head"),
        P("head"),
        P("ctx"),
    )
    return jax.shard_map(
        local,
        mesh=mesh,
        in_specs=placed,
        out_specs=(P("ctx"), P("ctx", "head"), P("ctx", "head"), P("ctx", "head"), P("head")),
        check_vma=False,
    )
```

profile of v0, /device:TPU:1, one launch (start us, length us, event | category | flops | bytes accessed | tf_op | source)
XLA Modules:
  0.0 164.8 jit_solution(1753874341078606613)
XLA Ops:
  0.6 0.8 reshape.214
  1.4 1.2 reduce-window.6
  2.6 0.2 slice_reduce_fusion
  2.8 0.2 reduce-window.9
  3.0 0.1 add_bitcast_fusion
  3.1 0.1 copy.225
  3.2 0.6 broadcast_in_dim.60
  3.9 17.1 %all-to-all-start = ((f32[64,1,4]{2,1,0:T(1,128)}), f32[64,1,4]{2,1,0:T(1,128)S(1)}, u32[]{:S(2)}, u32[]{:S(2)}) async-start(f32[64,1,4]{2,1,0:T(1,128)} %broadcast_in_dim.60), calls=%async_computation | async-start | bytes 65536 | tf_op jit(solution)/shard_map/all_to_all | solution.py:15
  21.0 0.1 multiply_bitcast_fusion
  21.1 0.1 iota_compare_fusion
  21.2 1.3 copy.185
  22.4 1.4 copy.184
  23.9 1.0 fusion.16
  24.9 2.8 %multiply_convert_fusion.1 = bf16[4,512,512]{2,1,0:T(8,128)(2,1)S(1)} fusion(bf16[512,4,128]{0,2,1:T(8,128)(2,1)S(1)} %bitcast.125, bf16[512,4,128]{0,2,1:T(8,128)(2,1)} %bitcast.130, f32[4,512]{1,0:T(4,128)S(1)} %bitcast.143, pred[512,512]{1,0:T(8,128)(4,1)S(1)} %iota_compare_fusion), kind=kOutput, calls=%fused_computation.1 | convolution fusion | flops 274726912 | bytes 3416064 | tf_op jit(solution)/shard_map/thd,shd->hts/dot_general | solution.py:102
  27.7 4.0 %all-to-all-done = f32[64,1,4]{2,1,0:T(1,128)S(1)} async-done(((f32[64,1,4]{2,1,0:T(1,128)}), f32[64,1,4]{2,1,0:T(1,128)S(1)}, u32[]{:S(2)}, u32[]{:S(2)}) %all-to-all-start) | async-done | bytes 1056 | tf_op jit(solution)/shard_map/all_to_all | solution.py:15
  31.8 8.4 %all-to-all-start.1 = ((f32[64,1,1024]{2,1,0:T(1,128)}), f32[64,1,1024]{2,1,0:T(1,128)}, u32[]{:S(2)}, u32[]{:S(2)}) async-start(f32[64,1,1024]{2,1,0:T(1,128)} %bitcast.137), calls=%async_computation.1 | async-start | bytes 524288 | tf_op jit(solution)/shard_map/all_to_all | solution.py:51
  40.3 0.1 copy.191
  40.4 0.1 reduce_window_sum.37
  40.6 11.9 %all-to-all-done.1 = f32[64,1,1024]{2,1,0:T(1,128)} async-done(((f32[64,1,1024]{2,1,0:T(1,128)}), f32[64,1,1024]{2,1,0:T(1,128)}, u32[]{:S(2)}, u32[]{:S(2)}) %all-to-all-start.1) | async-done | bytes 262176 | tf_op jit(solution)/shard_map/all_to_all | solution.py:51
  52.5 2.7 %fusion.11 = bf16[64,1024]{1,0:T(8,128)(2,1)} fusion(f32[4,1024]{1,0:T(4,128)S(1)} %fusion.48, f32[64,1,1024]{2,1,0:T(1,128)} %all-to-all-done.1, f32[4,64]{1,0:T(4,128)S(1)} %bitcast.145, f32[4,64]{1,0:T(4,128)S(1)} %bitcast_subtract_fusion, pred[64,64]{1,0:T(8,128)(4,1)S(1)} %iota_compare_fusion.2), kind=kOutput, calls=%fused_computation.27 | convolution fusion | flops 201834496 | bytes 415744 | tf_op jit(solution)/shard_map/hbc,cf->hbf/dot_general | solution.py:62
  55.2 0.6 broadcast.129
  55.8 1.6 reduce.8
  57.4 0.7 reshape.229
  58.1 6.2 %all-to-all-start.2 = ((bf16[64,2,512]{2,1,0:T(2,128)(2,1)}), bf16[64,2,512]{2,1,0:T(2,128)(2,1)S(1)}, u32[]{:S(2)}, u32[]{:S(2)}) async-start(bf16[64,2,512]{2,1,0:T(2,128)(2,1)} %reshape.229), calls=%async_computation.2 | async-start | bytes 262144 | tf_op jit(solution)/shard_map/all_to_all | solution.py:67
  64.3 1.8 %convolution_bitcast_fusion.3 = f32[512,4,128]{0,2,1:T(8,128)} fusion(bf16[4,512,512]{2,1,0:T(8,128)(2,1)S(1)} %multiply_convert_fusion.1, bf16[512,512]{1,0:T(8,128)(2,1)S(1)} %copy-done), kind=kOutput, calls=%fused_computation.9 | convolution fusion | flops 268435456 | bytes 3670016 | tf_op jit(solution)/shard_map/hts,shd->thd/dot_general | solution.py:104
  66.1 9.7 %all-to-all-done.2 = bf16[64,2,512]{2,1,0:T(2,128)(2,1)S(1)} async-done(((bf16[64,2,512]{2,1,0:T(2,128)(2,1)}), bf16[64,2,512]{2,1,0:T(2,128)(2,1)S(1)}, u32[]{:S(2)}, u32[]{:S(2)}) %all-to-all-start.2) | async-done | bytes 131104 | tf_op jit(solution)/shard_map/all_to_all | solution.py:67
  75.8 0.1 reshape.230
  75.9 0.7 reduce.5
  76.8 2.4 %multiply_reduce_fusion.2 = (f32[512]{0:T(512)}, f32[512]{0:T(512)}, f32[512,4,128]{0,2,1:T(8,128)S(1)}) fusion(f32[4,128]{1,0:T(4,128)} %bitcast.140, f32[512,4,128]{0,2,1:T(8,128)} %convolution_bitcast_fusion.3, bf16[4,128,128]{2,1,0:T(8,128)(2,1)S(1)} %reshape.218, bf16[512,4,128]{0,2,1:T(8,128)(2,1)S(1)} %bitcast.126, f32[512,4]{0,1:T(4,128)S(1)} %get-tuple-element.49), kind=kOutput, calls=%fused_computation.36 | convolution fusion | flops 68942848 | bytes 2766848 | tf_op jit(solution)/shard_map/thd,hde->the/dot_general | solution.py:107
  79.1 0.3 copy.198
  79.5 1.0 fusion.13
  80.4 0.7 pad_maximum_fusion
  81.2 0.7 broadcast_in_dim.62
  81.8 7.5 %all-to-all-start.3 = ((f32[8,1,2048]{2,1,0:T(1,128)}), f32[8,1,2048]{2,1,0:T(1,128)S(1)}, u32[]{:S(2)}, u32[]{:S(2)}) async-start(f32[8,1,2048]{2,1,0:T(1,128)} %broadcast_in_dim.62), calls=%async_computation.3 | async-start | bytes 131072 | tf_op jit(solution)/shard_map/all_to_all | solution.py:15
  89.3 0.6 iota_compare_fusion.1
  89.9 4.2 %all-to-all-done.3 = f32[8,1,2048]{2,1,0:T(1,128)S(1)} async-done(((f32[8,1,2048]{2,1,0:T(1,128)}), f32[8,1,2048]{2,1,0:T(1,128)S(1)}, u32[]{:S(2)}, u32[]{:S(2)}) %all-to-all-start.3) | async-done | bytes 65568 | tf_op jit(solution)/shard_map/all_to_all | solution.py:15
  94.2 1.3 fusion.54
  95.5 1.8 %multiply_reduce_fusion = (f32[512]{0:T(512)}, bf16[512,512]{1,0:T(8,128)(2,1)S(1)}) fusion(bf16[512,512]{1,0:T(8,128)(2,1)S(1)} %copy-done.7, f32[512]{0:T(512)} %param.13, f32[512]{0:T(512)} %param.12, f32[512,512]{1,0:T(8,128)S(1)} %copy.198, f32[512]{0:T(512)S(1)} %get-tuple-element.46, f32[512]{0:T(512)S(1)} %get-tuple-element.47), kind=kLoop, calls=%fused_computation.32 | loop fusion | flops 3145216 | bytes 2107392 | tf_op jit(solution)/shard_map/reduce_sum | solution.py:143
  97.3 0.2 copy.230
  97.5 3.1 %convolution_bitcast_fusion.1 = f32[512,4,128]{0,2,1:T(8,128)} fusion(bf16[512,4,128]{0,2,1:T(8,128)(2,1)S(1)} %bitcast.121, bf16[4,512,512]{2,1,0:T(8,128)(2,1)} %copy-done.1), kind=kOutput, calls=%fused_computation.7 | convolution fusion | flops 268435456 | bytes 3670016 | tf_op jit(solution)/shard_map/hts,the->she/dot_general | solution.py:164
  100.6 1.0 fusion.17
  101.6 1.8 %multiply_convert_fusion = bf16[4,512,512]{2,1,0:T(8,128)(2,1)S(1)} fusion(bf16[512,4,128]{0,2,1:T(8,128)(2,1)S(1)} %bitcast.123, f32[4,512]{1,0:T(4,128)S(1)} %bitcast.144, pred[512,512]{1,0:T(8,128)(4,1)S(1)} %iota_compare_fusion, bf16[512,512]{1,0:T(8,128)(2,1)S(1)} %copy-done), kind=kOutput, calls=%fused_computation | convolution fusion | flops 274726912 | bytes 3416064 | tf_op jit(solution)/shard_map/the,she->hts/dot_general | solution.py:150
  103.4 4.8 %all-to-all-start.4 = ((f32[64,1,1024]{2,1,0:T(1,128)}), f32[64,1,1024]{2,1,0:T(1,128)S(1)}, u32[]{:S(2)}, u32[]{:S(2)}) async-start(f32[64,1,1024]{2,1,0:T(1,128)} %bitcast.18), calls=%async_computation.4 | async-start | bytes 524288 | tf_op jit(solution)/shard_map/all_to_all | solution.py:51
  108.3 1.3 broadcast_multiply_fusion
  109.5 2.8 %convolution_bitcast_fusion.2 = f32[512,4,128]{0,2,1:T(8,128)} fusion(bf16[4,512,512]{2,1,0:T(8,128)(2,1)S(1)} %multiply_convert_fusion, bf16[512,4,128]{0,2,1:T(8,128)(2,1)} %bitcast.131), kind=kOutput, calls=%fused_computation.8 | convolution fusion | flops 268435456 | bytes 3670016 | tf_op jit(solution)/shard_map/hts,shd->thd/dot_general | solution.py:154
  112.4 8.9 %all-to-all-done.4 = f32[64,1,1024]{2,1,0:T(1,128)S(1)} async-done(((f32[64,1,1024]{2,1,0:T(1,128)}), f32[64,1,1024]{2,1,0:T(1,128)S(1)}, u32[]{:S(2)}, u32[]{:S(2)}) %all-to-all-start.4) | async-done | bytes 262176 | tf_op jit(solution)/shard_map/all_to_all | solution.py:51
  121.3 1.4 broadcast_in_dim.111
  122.7 5.5 %all-to-all-start.6 = ((f32[64,1,512]{2,1,0:T(1,128)}), f32[64,1,512]{2,1,0:T(1,128)S(1)}, u32[]{:S(2)}, u32[]{:S(2)}) async-start(f32[64,1,512]{2,1,0:T(1,128)} %broadcast_in_dim.111), calls=%async_computation.6 | async-start | bytes 262144 | tf_op jit(solution)/shard_map/all_to_all | solution.py:15
  128.2 2.3 %fusion.8 = bf16[512,4,128]{0,2,1:T(8,128)(2,1)} fusion(f32[512,4,128]{0,2,1:T(8,128)} %convolution_bitcast_fusion.2, bf16[4,128,128]{2,1,0:T(8,128)(2,1)S(1)} %reshape.218, bf16[512,4,128]{0,2,1:T(8,128)(2,1)S(1)} %bitcast.124, f32[512,4]{0,1:T(4,128)S(1)} %get-tuple-element.49), kind=kOutput, calls=%fused_computation.24 | convolution fusion | flops 67895296 | bytes 2236416 | tf_op jit(solution)/shard_map/the,hde->thd/dot_general | solution.py:156
  130.5 2.1 %copy.212 = bf16[512,512]{1,0:T(8,128)(2,1)} copy(bf16[512,512]{0,1:T(8,128)(2,1)} %bitcast.134) | data formatting | bytes 1048576
  132.6 2.0 %fusion.12 = bf16[64,1024]{1,0:T(8,128)(2,1)S(1)} fusion(f32[4,1024]{1,0:T(4,128)} %copy-done.9, f32[64,1,1024]{2,1,0:T(1,128)} %copy-done.8, f32[4,64]{1,0:T(4,128)} %bitcast.146, f32[4,64]{1,0:T(4,128)} %copy-done.13, pred[64,64]{1,0:T(8,128)(4,1)} %iota_compare_fusion.1), kind=kOutput, calls=%fused_computation.28 | convolution fusion | flops 201834496 | bytes 415744 | tf_op jit(solution)/shard_map/hbc,cf->hbf/dot_general | solution.py:62
  134.7 0.7 reduce.9
  135.4 0.7 reshape.231
  136.1 3.6 %all-to-all-done.6 = f32[64,1,512]{2,1,0:T(1,128)S(1)} async-done(((f32[64,1,512]{2,1,0:T(1,128)}), f32[64,1,512]{2,1,0:T(1,128)S(1)}, u32[]{:S(2)}, u32[]{:S(2)}) %all-to-all-start.6) | async-done | bytes 131104 | tf_op jit(solution)/shard_map/all_to_all | solution.py:15
  139.7 8.5 %all-to-all-start.5 = ((bf16[64,2,512]{2,1,0:T(2,128)(2,1)}), bf16[64,2,512]{2,1,0:T(2,128)(2,1)S(1)}, u32[]{:S(2)}, u32[]{:S(2)}) async-start(bf16[64,2,512]{2,1,0:T(2,128)(2,1)} %reshape.231), calls=%async_computation.5 | async-start | bytes 262144 | tf_op jit(solution)/shard_map/all_to_all | solution.py:67
  148.3 1.4 convolution_bitcast_fusion
  149.7 0.7 reduce_sum.89
  150.4 9.4 %all-to-all-done.5 = bf16[64,2,512]{2,1,0:T(2,128)(2,1)S(1)} async-done(((bf16[64,2,512]{2,1,0:T(2,128)(2,1)}), bf16[64,2,512]{2,1,0:T(2,128)(2,1)S(1)}, u32[]{:S(2)}, u32[]{:S(2)}) %all-to-all-start.5) | async-done | bytes 131104 | tf_op jit(solution)/shard_map/all_to_all | solution.py:67
  159.8 0.1 reshape.232
  159.9 0.7 reduce.6
  160.8 1.7 %fusion.10 = bf16[512,4,128]{0,2,1:T(8,128)(2,1)S(1)} fusion(f32[512,4,128]{0,2,1:T(8,128)} %convolution_bitcast_fusion.1, bf16[4,128,128]{2,1,0:T(8,128)(2,1)S(1)} %reshape.221, bf16[512,4,128]{0,2,1:T(8,128)(2,1)} %bitcast.132, f32[512,4]{0,1:T(4,128)S(1)} %get-tuple-element.50), kind=kOutput, calls=%fused_computation.26 | convolution fusion | flops 67895296 | bytes 2236416 | tf_op jit(solution)/shard_map/shd,hde->she/dot_general | solution.py:166
  162.5 1.0 copy.214
  163.5 0.3 fusion.9
  163.8 1.0 copy.213
  (39 shorter events, 0.5 us)
Async XLA Ops:
  0.6 23.3 %copy-start = (bf16[512,512]{1,0:T(8,128)(2,1)S(1)}, bf16[512,512]{1,0:T(8,128)(2,1)}, u32[]{:S(2)}) copy-start(bf16[512,512]{1,0:T(8,128)(2,1)} %param.9) | copy-start | bytes 1572868
  3.0 24.7 %copy-start.10 = (f32[1,4,4,128]{3,1,2,0:T(4,128)}, f32[1,4,4,128]{3,1,2,0:T(4,128)S(1)}, u32[]{:S(2)}) copy-start(f32[1,4,4,128]{3,1,2,0:T(4,128)S(1)} %copy.262) | copy-start | bytes 24580
  3.9 27.9 %all-to-all-start = ((f32[64,1,4]{2,1,0:T(1,128)}), f32[64,1,4]{2,1,0:T(1,128)S(1)}, u32[]{:S(2)}, u32[]{:S(2)}) async-start(f32[64,1,4]{2,1,0:T(1,128)} %broadcast_in_dim.60), calls=%async_computation | async-start | bytes 65536 | tf_op jit(solution)/shard_map/all_to_all | solution.py:15
  22.4 2.5 %copy-start.5 = (bf16[512,512]{0,1:T(8,128)(2,1)}, bf16[512,512]{0,1:T(8,128)(2,1)S(1)}, u32[]{:S(2)}) copy-start(bf16[512,512]{0,1:T(8,128)(2,1)S(1)} %copy.185) | copy-start | bytes 1572868
  23.9 52.9 %copy-start.2 = (bf16[512,512]{0,1:T(8,128)(2,1)}, bf16[512,512]{0,1:T(8,128)(2,1)S(1)}, u32[]{:S(2)}) copy-start(bf16[512,512]{0,1:T(8,128)(2,1)S(1)} %copy.184) | copy-start | bytes 1572868
  27.7 38.4 %copy-start.1 = (bf16[4,512,512]{2,1,0:T(8,128)(2,1)}, bf16[4,512,512]{2,1,0:T(8,128)(2,1)S(1)}, u32[]{:S(2)}) copy-start(bf16[4,512,512]{2,1,0:T(8,128)(2,1)S(1)} %multiply_convert_fusion.1) | copy-start | bytes 6291460
  31.8 20.7 %all-to-all-start.1 = ((f32[64,1,1024]{2,1,0:T(1,128)}), f32[64,1,1024]{2,1,0:T(1,128)}, u32[]{:S(2)}, u32[]{:S(2)}) async-start(f32[64,1,1024]{2,1,0:T(1,128)} %bitcast.137), calls=%async_computation.1 | async-start | bytes 524288 | tf_op jit(solution)/shard_map/all_to_all | solution.py:51
  40.2 15.0 %copy-start.9 = (f32[4,1024]{1,0:T(4,128)}, f32[4,1024]{1,0:T(4,128)S(1)}, u32[]{:S(2)}) copy-start(f32[4,1024]{1,0:T(4,128)S(1)} %fusion.48) | copy-start | bytes 49156
  40.6 14.6 %copy-start.12 = (f32[64,4]{0,1:T(4,128)}, f32[64,4]{0,1:T(4,128)S(1)}, u32[]{:S(2)}) copy-start(f32[64,4]{0,1:T(4,128)S(1)} %copy.192) | copy-start | bytes 3076
  40.6 14.6 %copy-start.13 = (f32[4,64]{1,0:T(4,128)}, f32[4,64]{1,0:T(4,128)S(1)}, u32[]{:S(2)}) copy-start(f32[4,64]{1,0:T(4,128)S(1)} %bitcast_subtract_fusion) | copy-start | bytes 3076
  58.1 17.7 %all-to-all-start.2 = ((bf16[64,2,512]{2,1,0:T(2,128)(2,1)}), bf16[64,2,512]{2,1,0:T(2,128)(2,1)S(1)}, u32[]{:S(2)}, u32[]{:S(2)}) async-start(bf16[64,2,512]{2,1,0:T(2,128)(2,1)} %reshape.229), calls=%async_computation.2 | async-start | bytes 262144 | tf_op jit(solution)/shard_map/all_to_all | solution.py:67
  76.8 2.7 %copy-start.7 = (bf16[512,512]{1,0:T(8,128)(2,1)S(1)}, bf16[512,512]{1,0:T(8,128)(2,1)}, u32[]{:S(2)}) copy-start(bf16[512,512]{1,0:T(8,128)(2,1)} %param.11) | copy-start | bytes 1572868
  81.8 12.3 %all-to-all-start.3 = ((f32[8,1,2048]{2,1,0:T(1,128)}), f32[8,1,2048]{2,1,0:T(1,128)S(1)}, u32[]{:S(2)}, u32[]{:S(2)}) async-start(f32[8,1,2048]{2,1,0:T(1,128)} %broadcast_in_dim.62), calls=%async_computation.3 | async-start | bytes 131072 | tf_op jit(solution)/shard_map/all_to_all | solution.py:15
  97.5 3.1 %copy-start.3 = (bf16[512,512]{0,1:T(8,128)(2,1)S(1)}, bf16[512,512]{0,1:T(8,128)(2,1)}, u32[]{:S(2)}) copy-start(bf16[512,512]{0,1:T(8,128)(2,1)} %copy-done.2) | copy-start | bytes 1572868
  97.5 4.1 %copy-start.11 = (f32[1,4,4,128]{3,1,2,0:T(4,128)S(1)}, f32[1,4,4,128]{3,1,2,0:T(4,128)}, u32[]{:S(2)}) copy-start(f32[1,4,4,128]{3,1,2,0:T(4,128)} %copy-done.10) | copy-start | bytes 24580
  103.4 17.8 %all-to-all-start.4 = ((f32[64,1,1024]{2,1,0:T(1,128)}), f32[64,1,1024]{2,1,0:T(1,128)S(1)}, u32[]{:S(2)}, u32[]{:S(2)}) async-start(f32[64,1,1024]{2,1,0:T(1,128)} %bitcast.18), calls=%async_computation.4 | async-start | bytes 524288 | tf_op jit(solution)/shard_map/all_to_all | solution.py:51
  121.3 1.4 copy-start.8
  122.7 17.1 %all-to-all-start.6 = ((f32[64,1,512]{2,1,0:T(1,128)}), f32[64,1,512]{2,1,0:T(1,128)S(1)}, u32[]{:S(2)}, u32[]{:S(2)}) async-start(f32[64,1,512]{2,1,0:T(1,128)} %broadcast_in_dim.111), calls=%async_computation.6 | async-start | bytes 262144 | tf_op jit(solution)/shard_map/all_to_all | solution.py:15
  130.5 17.7 %copy-start.4 = (bf16[512,512]{0,1:T(8,128)(2,1)S(1)}, bf16[512,512]{0,1:T(8,128)(2,1)}, u32[]{:S(2)}) copy-start(bf16[512,512]{0,1:T(8,128)(2,1)} %copy-done.2) | copy-start | bytes 1572868
  139.7 20.1 %all-to-all-start.5 = ((bf16[64,2,512]{2,1,0:T(2,128)(2,1)}), bf16[64,2,512]{2,1,0:T(2,128)(2,1)S(1)}, u32[]{:S(2)}, u32[]{:S(2)}) async-start(bf16[64,2,512]{2,1,0:T(2,128)(2,1)} %reshape.231), calls=%async_computation.5 | async-start | bytes 262144 | tf_op jit(solution)/shard_map/all_to_all | solution.py:67
  150.4 13.1 %copy-start.6 = (f32[512,4,128]{0,2,1:T(8,128)S(1)}, f32[512,4,128]{0,2,1:T(8,128)}, u32[]{:S(2)}) copy-start(f32[512,4,128]{0,2,1:T(8,128)} %convolution_bitcast_fusion) | copy-start | bytes 3145732
where the time goes:
time: 167 us; the launch traced here: 165 us
  starting transfers between devices  58.1 us (35%)
  waiting for transfers between devices  51.9 us (31%)
  matrix products  27.2 us (16%)
  local copies, waits for them, and re-layouts  13.8 us (8%)
  other arithmetic  12.9 us (8%)
    all_to_all x3, starting transfers between devices, sent_to_all(): lax.all_to_all(jnp.broadcast_to(shard[None], (devices, *shard.shape)), ax...  30.2 us
    all_to_all x2, waiting for transfers between devices, owner_prefix(): lax.all_to_all(outgoing, 'ctx', split_axis=0, concat_axis=0, tiled=True)  20.8 us
    all_to_all x2, waiting for transfers between devices, owner_prefix(): lax.all_to_all(combined, 'ctx', split_axis=0, concat_axis=0, tiled=True)  19.1 us
    all_to_all x2, starting transfers between devices, owner_prefix(): lax.all_to_all(combined, 'ctx', split_axis=0, concat_axis=0, tiled=True)  14.7 us
    all_to_all x2, starting transfers between devices, owner_prefix(): lax.all_to_all(outgoing, 'ctx', split_axis=0, concat_axis=0, tiled=True)  13.2 us
    all_to_all x3, waiting for transfers between devices, sent_to_all(): lax.all_to_all(jnp.broadcast_to(shard[None], (devices, *shard.shape)), ax...  11.9 us
    unnamed x39, local copies, waits for them, and re-layouts  8.65 us
    dot_general x2, matrix products, owner_prefix(): jnp.einsum('hbc,cf->hbf', weights, spread, precision=lax.Precision.HIGHEST)  4.69 us
  transfers between devices with their start and end apart: 7, of which 7 were waited for; matrix products, arithmetic and copies ran while one was open for 14% of the time, Pallas kernels for 0%

commit v1 on v0

v1 whole, which is shorter than its diff:
```python
import jax
import jax.numpy as jnp
from jax import lax
from jax.experimental import pallas as pl
from jax.experimental.pallas import tpu as pltpu
from jax.sharding import PartitionSpec as P

HEAD_DIM = 128
HIDDEN_DIMENSION = 4096
EPS = 1e-06
SCALE = HEAD_DIM ** (-0.5)
TOK = 512
HEADS = 4
BLOCKS = 64
PER_HEAD = BLOCKS // HEADS
HALF = TOK // 2
FAR = -1e9

F32 = jnp.float32
BF16 = jnp.bfloat16

NN = (((1,), (0,)), ((), ()))
NT = (((1,), (1,)), ((), ()))
TN = (((0,), (0,)), ((), ()))


def mm(a, b, dims=NN):
    return lax.dot_general(a, b, dims, preferred_element_type=F32)


def head(h):
    return slice(h * HEAD_DIM, (h + 1) * HEAD_DIM)


def pieces(x):
    hi = x.astype(BF16).astype(F32)
    rest = x - hi
    mid = rest.astype(BF16).astype(F32)
    return hi, mid, rest - mid


def aux_tile(row):
    hi, mid, lo = pieces(row)
    at = lax.broadcasted_iota(jnp.int32, (8, HEAD_DIM), 0)
    return jnp.where(at == 0, hi, jnp.where(at == 1, mid, jnp.where(at == 2, lo, 0.0)))


def message(matrix, row):
    data = matrix.reshape(PER_HEAD, 8, HEAD_DIM)
    aux = jnp.broadcast_to(aux_tile(row)[None], (PER_HEAD, 8, HEAD_DIM))
    return jnp.concatenate([data, aux], axis=1).astype(BF16)


def summary_kernel(retention, keys, values, out, cum_out):
    rows = jnp.concatenate([retention[...], jnp.zeros((8 - HEADS, TOK), F32)], axis=0)
    parts = pieces(rows)
    stacked = jnp.concatenate(
        [p[:, c * 128 : (c + 1) * 128] for c in range(TOK // 128) for p in parts], axis=0
    ).astype(BF16)
    first = lax.broadcasted_iota(jnp.int32, (128, 128), 0)
    second = lax.broadcasted_iota(jnp.int32, (128, 128), 1)
    upper = jnp.where(first <= second, 1.0, 0.0).astype(BF16)
    sums = mm(stacked, upper)
    offset = jnp.zeros((8, 1), F32)
    chunks = []
    for c in range(TOK // 128):
        own = sums[24 * c : 24 * c + 8] + sums[24 * c + 8 : 24 * c + 16] + sums[24 * c + 16 : 24 * c + 24]
        own = own + offset
        offset = own[:, 127:128]
        chunks.append(own)
    cum = jnp.concatenate(chunks, axis=1)
    cum_out[...] = cum
    tail = jnp.exp(offset - cum)
    decay = jnp.broadcast_to(jnp.exp(offset), (8, HEAD_DIM))
    for h in range(HEADS):
        turned = keys[:, head(h)].T
        key_decayed = (turned.astype(F32) * tail[h : h + 1]).astype(BF16)
        out[h * PER_HEAD : (h + 1) * PER_HEAD] = message(
            mm(key_decayed, values[:, head(h)]), decay[h : h + 1]
        )


def decay_rows(aux):
    return jnp.broadcast_to(aux[0:1] + aux[1:2] + aux[2:3], (8, HEAD_DIM))


def forward_scan_kernel(arrived, out):
    state = jnp.zeros((8, HEAD_DIM), F32)
    for pair in range(BLOCKS // 2):
        both = []
        for b in (2 * pair, 2 * pair + 1):
            both.append(state)
            got = arrived[b].astype(F32)
            state = decay_rows(got[8:16]) * state + got[0:8]
        out[16 * pair : 16 * pair + 16] = jnp.concatenate(both, axis=0).astype(BF16)


def backward_scan_kernel(arrived, decays, out):
    gain = jnp.zeros((8, HEAD_DIM), F32)
    for b in range(BLOCKS):
        gain = gain + arrived[b].astype(F32)[8:16]
    aux = aux_tile(gain[0:1] + gain[1:2] + gain[2:3])
    state = jnp.zeros((8, HEAD_DIM), F32)
    for b in reversed(range(BLOCKS)):
        out[b] = jnp.concatenate([state, aux], axis=0).astype(BF16)
        state = decay_rows(decays[b].astype(F32)[8:16]) * state + arrived[b].astype(F32)[0:8]


def block_decay(cum, columns, h, i):
    rows, width = slice(i * HALF, (i + 1) * HALF), (i + 1) * HALF
    gap = columns[rows, h : h + 1] - cum[h : h + 1, 0:width]
    t = lax.broadcasted_iota(jnp.int32, (HALF, width), 0) + i * HALF
    s = lax.broadcasted_iota(jnp.int32, (HALF, width), 1)
    return jnp.exp(jnp.where(s <= t, gap, FAR))


def local_kernel(queries, keys, values, target, cum, local, probs, turned, columns, target_square):
    total = cum[:, TOK - 1 : TOK]
    start = jnp.exp(cum[...]) * SCALE
    tail = jnp.exp(total - cum[...])
    side = jnp.concatenate([cum[...], start, tail, jnp.zeros((104, TOK), F32)], axis=0).T
    columns[...] = side
    square = jnp.zeros((TOK, HEAD_DIM), F32)
    for h in range(HEADS):
        x = target[:, head(h)].astype(F32)
        square = square + x * x
        q, k, v = queries[:, head(h)], keys[:, head(h)], values[:, head(h)]
        turned[head(h), :] = (q.T.astype(F32) * start[h : h + 1]).astype(BF16)
        for i in range(2):
            rows, width = slice(i * HALF, (i + 1) * HALF), (i + 1) * HALF
            scores = mm(q[rows], k[0:width], NT)
            p = (scores * SCALE * block_decay(cum, side, h, i)).astype(BF16)
            probs[h, rows, 0:width] = p
            local[rows, head(h)] = mm(p, v[0:width])
    target_square[...] = jnp.sum(square.T, axis=0, keepdims=True)


def output_kernel(queries, states, local, columns, target, gain, target_square, attn, sums):
    square = jnp.zeros((TOK, HEAD_DIM), F32)
    gain_square = square
    cross = square
    for h in range(HEADS):
        carried = mm(queries[:, head(h)], states[head(h), :])
        o = local[:, head(h)] + columns[:, 8 + h : 9 + h] * carried
        attn[:, head(h)] = o
        gained = gain[:, head(h)] * o
        square = square + o * o
        gain_square = gain_square + gained * gained
        cross = cross + gained * target[:, head(h)].astype(F32)
    four = jnp.concatenate(
        [jnp.sum(a.T, axis=0, keepdims=True) for a in (square, gain_square, cross)]
        + [target_square[...]],
        axis=0,
    )
    for d in range(8):
        sums[d] = four


def gradient_kernel(sums, attn, target, gain, weight, turned, out, grad_out, payoff):
    four = jnp.sum(sums[...], axis=0)
    mean_square = four[0:1] / HIDDEN_DIMENSION + EPS
    inverse = 1.0 / jnp.sqrt(mean_square)
    pred_square = four[1:2] / mean_square
    pred_cross = four[2:3] * inverse
    payoff[...] = (pred_square - 2.0 * pred_cross + four[3:4]) / HIDDEN_DIMENSION
    inner = weight[...] * (pred_square - pred_cross)
    a = weight[...] / mean_square
    b = weight[...] * inverse
    c = inner / (HIDDEN_DIMENSION * mean_square)
    side = jnp.concatenate([a, b, c, jnp.zeros((125, TOK), F32)], axis=0).T
    a, b, c = side[:, 0:1], side[:, 1:2], side[:, 2:3]
    for h in range(HEADS):
        o, x, g = attn[:, head(h)], target[:, head(h)].astype(F32), gain[:, head(h)]
        error = a * (g * o) - b * x
        gain_row = jnp.sum(error * o, axis=0, keepdims=True)
        d = (error * g - c * o).astype(BF16)
        grad_out[:, head(h)] = d
        out[h * PER_HEAD : (h + 1) * PER_HEAD] = message(mm(turned[head(h), :], d), gain_row)


def local_gradient_kernel(
    grad_out, queries, keys, values, probs, states, cum, columns, grad_q, local_k, local_v
):
    for h in range(HEADS):
        q, k, v, d = queries[:, head(h)], keys[:, head(h)], values[:, head(h)], grad_out[:, head(h)]
        carried = columns[:, 8 + h : 9 + h] * mm(d, states[head(h), :], NT)
        parts = []
        for i in range(2):
            rows, width = slice(i * HALF, (i + 1) * HALF), (i + 1) * HALF
            grads = mm(d[rows], v[0:width], NT)
            gp = (grads * SCALE * block_decay(cum, columns, h, i)).astype(BF16)
            parts.append(gp)
            grad_q[rows, head(h)] = (mm(gp, k[0:width]) + carried[rows]).astype(BF16)
        early = jnp.concatenate([parts[0], parts[1][:, 0:HALF]], axis=0)
        local_k[0:HALF, head(h)] = mm(early, q, TN)
        local_k[HALF:TOK, head(h)] = mm(parts[1][:, HALF:TOK], q[HALF:TOK], TN)
        local_v[0:HALF, head(h)] = mm(probs[h, :, 0:HALF], d, TN)
        local_v[HALF:TOK, head(h)] = mm(probs[h, HALF:TOK, HALF:TOK], d[HALF:TOK], TN)


def final_kernel(arrived, keys, values, local_k, local_v, columns, grad_k, grad_v, gain_out):
    for h in range(HEADS):
        got = arrived[h * PER_HEAD : (h + 1) * PER_HEAD].astype(F32)
        state = got[:, 0:8].reshape(HEAD_DIM, HEAD_DIM).astype(BF16)
        aux = got[0, 8:16]
        gain_out[:, head(h)] = (aux[0:1] + aux[1:2] + aux[2:3]) / (BLOCKS * TOK)
        tail = columns[:, 16 + h : 17 + h]
        grad_k[:, head(h)] = (
            local_k[:, head(h)] + tail * mm(values[:, head(h)], state, NT)
        ).astype(BF16)
        grad_v[:, head(h)] = (
            local_v[:, head(h)] + tail * mm(keys[:, head(h)], state)
        ).astype(BF16)


def call(kernel, outs, args, flops, name):
    moved = sum(a.size * a.dtype.itemsize for a in args)
    moved += sum(o.size * o.dtype.itemsize for o in outs)
    whole = pl.BlockSpec(memory_space=pltpu.VMEM)
    return pl.pallas_call(
        kernel,
        out_shape=outs,
        in_specs=[whole] * len(args),
        out_specs=[whole] * len(outs),
        compiler_params=pltpu.CompilerParams(vmem_limit_bytes=32 * 2**20),
        cost_estimate=pl.CostEstimate(flops=flops, bytes_accessed=moved, transcendentals=0),
        name=name,
    )(*args)


def shape(dims, kind):
    return jax.ShapeDtypeStruct(dims, kind)


def exchange(x, axis):
    return lax.all_to_all(x, axis, 0, 0, tiled=True)


def local_part(queries, keys, values, retention, target, gain, weight):
    wide = TOK * TOK * HEAD_DIM * 2 * HEADS
    narrow = TOK * HEAD_DIM * HEAD_DIM * 2 * HEADS
    gain = gain.reshape(1, -1)
    weight = weight.reshape(1, -1)
    slices = shape((BLOCKS, 16, HEAD_DIM), BF16)
    full32 = shape((TOK, TOK), F32)
    full16 = shape((TOK, TOK), BF16)
    row = shape((1, TOK), F32)

    sent, cum = call(
        summary_kernel, [slices, shape((8, TOK), F32)], [retention, keys, values], narrow, "summary"
    )
    arrived = exchange(sent, "ctx")
    local, probs, turned, columns, target_square = call(
        local_kernel,
        [full32, shape((HEADS, TOK, TOK), BF16), full16, shape((TOK, 128), F32), row],
        [queries, keys, values, target, cum],
        2 * wide,
        "local",
    )
    [back] = call(forward_scan_kernel, [shape((TOK, HEAD_DIM), BF16)], [arrived], 1000, "forward_scan")
    states = exchange(back.reshape(BLOCKS, 8, HEAD_DIM), "ctx").reshape(TOK, HEAD_DIM)
    attn, sums = call(
        output_kernel,
        [full32, shape((8, 4, TOK), F32)],
        [queries, states, local, columns, target, gain, target_square],
        narrow,
        "output",
    )
    sums = exchange(sums, "head")
    sent, grad_out, payoff = call(
        gradient_kernel, [slices, full16, row], [sums, attn, target, gain, weight, turned], narrow, "gradient"
    )
    arrived_back = exchange(sent, "ctx")
    grad_q, local_k, local_v = call(
        local_gradient_kernel,
        [full16, full32, full32],
        [grad_out, queries, keys, values, probs, states, cum, columns],
        4 * wide,
        "local_gradient",
    )
    [back] = call(backward_scan_kernel, [slices], [arrived_back, arrived], 1000, "backward_scan")
    last = exchange(back, "ctx")
    grad_k, grad_v, gain_out = call(
        final_kernel,
        [full16, full16, row],
        [last, keys, values, local_k, local_v, columns],
        2 * narrow,
        "final",
    )
    return payoff.reshape(-1), grad_q, grad_k, grad_v, gain_out.reshape(-1)


def solution(mesh):
    placed = (
        P("ctx", "head"),
        P("ctx", "head"),
        P("ctx", "head"),
        P("head", "ctx"),
        P("ctx", "head"),
        P("head"),
        P("ctx"),
    )
    return jax.shard_map(
        local_part,
        mesh=mesh,
        in_specs=placed,
        out_specs=(P("ctx"), P("ctx", "head"), P("ctx", "head"), P("ctx", "head"), P("head")),
        check_vma=False,
    )
```

time: 167 us -> 110 us (0.66)
  blocking collectives: 0 us -> 58.6 us
  starting transfers between devices: 58.1 us -> 12 us
  waiting for transfers between devices: 51.9 us -> 12.2 us
  matrix products: 27.2 us -> 0 us
  other arithmetic: 12.9 us -> 0 us
  Pallas kernels: 0 us -> 11.1 us
    all_to_all x0 -> x3, blocking collectives: none -> 58.6 us  [exchange(): return lax.all_to_all(x, axis, 0, 0, tiled=True)]
    all_to_all x7 -> x2, starting transfers between devices: 58.1 us -> 12 us  [exchange(): return lax.all_to_all(x, axis, 0, 0, tiled=True)]
    all_to_all x7 -> x2, waiting for transfers between devices: 51.9 us -> 12.2 us  [exchange(): return lax.all_to_all(x, axis, 0, 0, tiled=True)]
    dot_general x14 -> x0, matrix products: 27.2 us -> none  [the longest x2 4.69 us: owner_prefix(): jnp.einsum('hbc,cf->hbf', weights, spread, precision=lax.Precision.HIGHEST)]
    pallas_call x0 -> x8, Pallas kernels: none -> 11.1 us  [call(): pl.pallas_call(kernel, out_shape=outs, in_specs=[whole] * len(args), out_...]
    unnamed x39 -> x38, local copies, waits for them, and re-layouts: 8.65 us -> 13.1 us
    reduce_sum x4 -> x0, other arithmetic: 3.5 us -> none  [the longest x1 1.79 us: local(): jnp.sum(discrepancy_adjoint * rescaled_activations, axis=0) / tokens_all]
    broadcast_in_dim x3 -> x0, local copies, waits for them, and re-layouts: 2.7 us -> none  [sent_to_all(): jnp.broadcast_to(shard[None], (devices, *shard.shape))]
  transfers between devices with their start and end apart: 7 -> 2, of which waited for: 7 -> 2; matrix products, arithmetic and copies ran while one was open for 14% -> 0% of each run, Pallas kernels for 0% -> 5%
where the time goes in v1:
time: 110 us; the launch traced here: 108 us
  blocking collectives  58.6 us (53%)
  local copies, waits for them, and re-layouts  13.1 us (12%)
  waiting for transfers between devices  12.2 us (11%)
  starting transfers between devices  12 us (11%)
  Pallas kernels  11.1 us (10%)
    all_to_all x3, blocking collectives, exchange(): return lax.all_to_all(x, axis, 0, 0, tiled=True)  58.6 us
    unnamed x38, local copies, waits for them, and re-layouts  13.1 us
    all_to_all x2, waiting for transfers between devices, exchange(): return lax.all_to_all(x, axis, 0, 0, tiled=True)  12.2 us
    all_to_all x2, starting transfers between devices, exchange(): return lax.all_to_all(x, axis, 0, 0, tiled=True)  12 us
    pallas_call x8, Pallas kernels, call(): pl.pallas_call(kernel, out_shape=outs, in_specs=[whole] * len(args), out_...  11.1 us
  transfers between devices with their start and end apart: 2, of which 2 were waited for; matrix products, arithmetic and copies ran while one was open for 0% of the time, Pallas kernels for 5%

profile of v1, /device:TPU:1, one launch (start us, length us, event | category | flops | bytes accessed | tf_op | source)
XLA Modules:
  0.0 107.9 jit_solution(652268860326921730)
XLA Ops:
  0.6 0.0 copy-start
  0.6 1.0 copy-done
  1.7 0.0 copy-start.2
  1.7 1.0 copy-done.2
  2.7 0.0 copy-start.16
  2.7 0.7 copy-done.16
  3.4 0.0 copy-start.1
  3.4 0.0 copy-start.3
  3.4 0.0 copy-start.4
  3.4 0.0 copy-start.5
  3.4 0.0 copy-start.17
  3.4 0.7 summary.1
  4.1 29.5 %all_to_all.25.arrived.decays = bf16[64,16,128]{2,1,0:T(8,128)(2,1)S(1)} all-to-all(bf16[64,16,128]{2,1,0:T(8,128)(2,1)S(1)} %get-tuple-element.23), channel_id=1, replica_groups=mesh['ctx'=64,'head'=8] {'ctx'}, dimensions={0} | all-to-all | bytes 524288 | tf_op jit(solution)/shard_map/all_to_all | solution.py:236
  33.6 0.8 forward_scan.1
  34.4 5.9 %all-to-all-start.1 = ((bf16[64,8,128]{2,1,0:T(8,128)(2,1)}), bf16[64,8,128]{2,1,0:T(8,128)(2,1)S(1)}, u32[]{:S(2)}, u32[]{:S(2)}) async-start(bf16[64,8,128]{2,1,0:T(8,128)(2,1)} %bitcast), calls=%async_computation.1 | async-start | bytes 262144 | tf_op jit(solution)/shard_map/all_to_all | solution.py:236
  40.3 0.0 copy-done.1
  40.3 0.0 copy-done.3
  40.3 0.0 copy-done.4
  40.3 0.0 copy-done.5
  40.4 0.0 copy-start.18
  40.4 1.7 %local.1 = (f32[512,512]{1,0:T(8,128)S(1)}, bf16[4,512,512]{2,1,0:T(8,128)(2,1)S(1)}, bf16[512,512]{1,0:T(8,128)(2,1)S(1)}, f32[512,128]{1,0:T(8,128)S(1)}, f32[1,512]{1,0:T(1,128)S(1)}) custom-call(bf16[512,512]{1,0:T(8,128)(2,1)S(1)} %copy-done.4, bf16[512,512]{1,0:T(8,128)(2,1)S(1)} %copy-done.1, bf16[512,512]{1,0:T(8,128)(2,1)S(1)} %copy-done.3, ...), custom_call_target="tpu_custom_call" | custom-call | flops 536870912 | bytes 6047744 | tf_op jit(solution)/shard_map/local/pallas_call | solution.py:220
  42.1 0.0 copy-start.6
  42.1 1.3 %copy-done.6 = bf16[4,512,512]{2,1,0:T(8,128)(2,1)} copy-done((bf16[4,512,512]{2,1,0:T(8,128)(2,1)}, bf16[4,512,512]{2,1,0:T(8,128)(2,1)S(1)}, u32[]{:S(2)}) %copy-start.6) | copy-done | bytes 2097176
  43.4 0.0 copy-start.12
  43.4 1.0 copy-done.12
  44.4 0.0 copy-start.14
  44.4 0.8 copy-done.14
  45.2 6.6 %all-to-all-done.1 = bf16[64,8,128]{2,1,0:T(8,128)(2,1)S(1)} async-done(((bf16[64,8,128]{2,1,0:T(8,128)(2,1)}), bf16[64,8,128]{2,1,0:T(8,128)(2,1)S(1)}, u32[]{:S(2)}, u32[]{:S(2)}) %all-to-all-start.1) | async-done | bytes 131104 | tf_op jit(solution)/shard_map/all_to_all | solution.py:236
  51.8 0.0 copy-done.17
  51.8 0.0 copy-start.13
  51.8 1.2 %copy-done.13 = f32[512,512]{1,0:T(8,128)S(1)} copy-done((f32[512,512]{1,0:T(8,128)S(1)}, f32[512,512]{1,0:T(8,128)}, u32[]{:S(2)}) %copy-start.13) | copy-done | bytes 1048600
  53.1 0.0 copy-start.15
  53.1 0.8 output.1
  53.8 12.3 %all_to_all.26.sums = f32[8,4,512]{2,1,0:T(4,128)S(1)} all-to-all(f32[8,4,512]{2,1,0:T(4,128)S(1)} %get-tuple-element.28), channel_id=1, replica_groups=mesh['ctx'=64,'head'=8] {'head'}, dimensions={0} | all-to-all | bytes 131072 | tf_op jit(solution)/shard_map/all_to_all | solution.py:236
  66.1 0.0 copy-done.18
  66.1 0.0 copy-done.15
  66.1 1.5 %gradient.1 = (bf16[64,16,128]{2,1,0:T(8,128)(2,1)S(1)}, bf16[512,512]{1,0:T(8,128)(2,1)S(1)}, f32[1,512]{1,0:T(1,128)}) custom-call(f32[8,4,512]{2,1,0:T(4,128)S(1)} %all_to_all.26.sums, f32[512,512]{1,0:T(8,128)S(1)} %get-tuple-element.29.attn, bf16[512,512]{1,0:T(8,128)(2,1)S(1)} %copy-done.5, f32[1,512]{1,0:T(1,128)S(1)} %bitcast.9, ...), custom_call_target="tpu_custom_call" | custom-call | flops 67108864 | bytes 2955264 | tf_op jit(solution)/shard_map/gradient/pallas_call | solution.py:220
  67.6 16.8 %all_to_all.27.arrived = bf16[64,16,128]{2,1,0:T(8,128)(2,1)S(1)} all-to-all(bf16[64,16,128]{2,1,0:T(8,128)(2,1)S(1)} %get-tuple-element.35), channel_id=1, replica_groups=mesh['ctx'=64,'head'=8] {'ctx'}, dimensions={0} | all-to-all | bytes 524288 | tf_op jit(solution)/shard_map/all_to_all | solution.py:236
  84.4 0.9 backward_scan.1
  85.3 6.2 %all-to-all-start.4 = ((bf16[64,16,128]{2,1,0:T(8,128)(2,1)}), bf16[64,16,128]{2,1,0:T(8,128)(2,1)S(1)}, u32[]{:S(2)}, u32[]{:S(2)}) async-start(bf16[64,16,128]{2,1,0:T(8,128)(2,1)} %backward_scan.1), calls=%async_computation.4 | async-start | bytes 524288 | tf_op jit(solution)/shard_map/all_to_all | solution.py:236
  91.5 0.0 copy-start.7
  91.5 1.6 %copy-done.7 = bf16[4,512,512]{2,1,0:T(8,128)(2,1)S(1)} copy-done((bf16[4,512,512]{2,1,0:T(8,128)(2,1)S(1)}, bf16[4,512,512]{2,1,0:T(8,128)(2,1)}, u32[]{:S(2)}) %copy-start.7) | copy-done | bytes 2097176
  93.1 3.4 %local_gradient.1 = (bf16[512,512]{1,0:T(8,128)(2,1)}, f32[512,512]{1,0:T(8,128)S(1)}, f32[512,512]{1,0:T(8,128)S(1)}) custom-call(bf16[512,512]{1,0:T(8,128)(2,1)S(1)} %get-tuple-element.32.grad_out, bf16[512,512]{1,0:T(8,128)(2,1)S(1)} %copy-done.4, bf16[512,512]{1,0:T(8,128)(2,1)S(1)} %copy-done.1, bf16[512,512]{1,0:T(8,128)(2,1)S(1)} %copy-done.3, ...), custom_call_target="tpu_custom_call" | custom-call | flops 1073741824 | bytes 7225344 | tf_op jit(solution)/shard_map/local_gradient/pallas_call | solution.py:220
  96.4 0.0 copy-start.8
  96.4 1.0 copy-done.8
  97.4 0.0 copy-start.10
  97.4 1.0 copy-done.10
  98.4 5.6 %all-to-all-done.4.arrived = bf16[64,16,128]{2,1,0:T(8,128)(2,1)S(1)} async-done(((bf16[64,16,128]{2,1,0:T(8,128)(2,1)}), bf16[64,16,128]{2,1,0:T(8,128)(2,1)S(1)}, u32[]{:S(2)}, u32[]{:S(2)}) %all-to-all-start.4) | async-done | bytes 262176 | tf_op jit(solution)/shard_map/all_to_all | solution.py:236
  104.0 0.0 copy-start.9
  104.0 1.2 %copy-done.9 = f32[512,512]{1,0:T(8,128)S(1)} copy-done((f32[512,512]{1,0:T(8,128)S(1)}, f32[512,512]{1,0:T(8,128)}, u32[]{:S(2)}) %copy-start.9) | copy-done | bytes 1048600
  105.2 0.0 copy-start.11
  105.2 1.2 %copy-done.11 = f32[512,512]{1,0:T(8,128)S(1)} copy-done((f32[512,512]{1,0:T(8,128)S(1)}, f32[512,512]{1,0:T(8,128)}, u32[]{:S(2)}) %copy-start.11) | copy-done | bytes 1048600
  106.4 1.5 %final.1 = (bf16[512,512]{1,0:T(8,128)(2,1)}, bf16[512,512]{1,0:T(8,128)(2,1)}, f32[1,512]{1,0:T(1,128)}) custom-call(bf16[64,16,128]{2,1,0:T(8,128)(2,1)S(1)} %all-to-all-done.4.arrived, bf16[512,512]{1,0:T(8,128)(2,1)S(1)} %copy-done.1, bf16[512,512]{1,0:T(8,128)(2,1)S(1)} %copy-done.3, f32[512,512]{1,0:T(8,128)S(1)} %copy-done.9, ...), custom_call_target="tpu_custom_call" | custom-call | flops 134217728 | bytes 4720640 | tf_op jit(solution)/shard_map/final/pallas_call | solution.py:220
Async XLA Ops:
  0.6 1.0 copy-start
  1.7 1.0 copy-start.2
  2.7 0.7 copy-start.16
  3.4 36.9 %copy-start.1 = (bf16[512,512]{1,0:T(8,128)(2,1)S(1)}, bf16[512,512]{1,0:T(8,128)(2,1)}, u32[]{:S(2)}) copy-start(bf16[512,512]{1,0:T(8,128)(2,1)} %keys.7) | copy-start | bytes 1572868
  3.4 36.9 %copy-start.3 = (bf16[512,512]{1,0:T(8,128)(2,1)S(1)}, bf16[512,512]{1,0:T(8,128)(2,1)}, u32[]{:S(2)}) copy-start(bf16[512,512]{1,0:T(8,128)(2,1)} %values.7) | copy-start | bytes 1572868
  3.4 36.9 %copy-start.4 = (bf16[512,512]{1,0:T(8,128)(2,1)S(1)}, bf16[512,512]{1,0:T(8,128)(2,1)}, u32[]{:S(2)}) copy-start(bf16[512,512]{1,0:T(8,128)(2,1)} %queries.5) | copy-start | bytes 1572868
  3.4 36.9 %copy-start.5 = (bf16[512,512]{1,0:T(8,128)(2,1)S(1)}, bf16[512,512]{1,0:T(8,128)(2,1)}, u32[]{:S(2)}) copy-start(bf16[512,512]{1,0:T(8,128)(2,1)} %target.5) | copy-start | bytes 1572868
  3.4 48.4 %copy-start.17 = (f32[512]{0:T(512)S(1)}, f32[512]{0:T(512)}, u32[]{:S(2)}) copy-start(f32[512]{0:T(512)} %param.12) | copy-start | bytes 6148
  34.4 17.4 %all-to-all-start.1 = ((bf16[64,8,128]{2,1,0:T(8,128)(2,1)}), bf16[64,8,128]{2,1,0:T(8,128)(2,1)S(1)}, u32[]{:S(2)}, u32[]{:S(2)}) async-start(bf16[64,8,128]{2,1,0:T(8,128)(2,1)} %bitcast), calls=%async_computation.1 | async-start | bytes 262144 | tf_op jit(solution)/shard_map/all_to_all | solution.py:236
  40.4 25.7 %copy-start.18 = (f32[512]{0:T(512)S(1)}, f32[512]{0:T(512)}, u32[]{:S(2)}) copy-start(f32[512]{0:T(512)} %param.13) | copy-start | bytes 6148
  42.1 1.3 %copy-start.6 = (bf16[4,512,512]{2,1,0:T(8,128)(2,1)}, bf16[4,512,512]{2,1,0:T(8,128)(2,1)S(1)}, u32[]{:S(2)}) copy-start(bf16[4,512,512]{2,1,0:T(8,128)(2,1)S(1)} %get-tuple-element.33.probs) | copy-start | bytes 6291460
  43.4 1.0 copy-start.12
  44.4 0.8 copy-start.14
  51.8 1.2 %copy-start.13 = (f32[512,512]{1,0:T(8,128)S(1)}, f32[512,512]{1,0:T(8,128)}, u32[]{:S(2)}) copy-start(f32[512,512]{1,0:T(8,128)} %copy-done.12) | copy-start | bytes 3145732
  53.1 13.1 %copy-start.15 = (bf16[512,512]{1,0:T(8,128)(2,1)S(1)}, bf16[512,512]{1,0:T(8,128)(2,1)}, u32[]{:S(2)}) copy-start(bf16[512,512]{1,0:T(8,128)(2,1)} %copy-done.14) | copy-start | bytes 1572868
  85.3 18.7 %all-to-all-start.4 = ((bf16[64,16,128]{2,1,0:T(8,128)(2,1)}), bf16[64,16,128]{2,1,0:T(8,128)(2,1)S(1)}, u32[]{:S(2)}, u32[]{:S(2)}) async-start(bf16[64,16,128]{2,1,0:T(8,128)(2,1)} %backward_scan.1), calls=%async_computation.4 | async-start | bytes 524288 | tf_op jit(solution)/shard_map/all_to_all | solution.py:236
  91.5 1.6 %copy-start.7 = (bf16[4,512,512]{2,1,0:T(8,128)(2,1)S(1)}, bf16[4,512,512]{2,1,0:T(8,128)(2,1)}, u32[]{:S(2)}) copy-start(bf16[4,512,512]{2,1,0:T(8,128)(2,1)} %copy-done.6) | copy-start | bytes 6291460
  96.4 1.0 copy-start.8
  97.4 1.0 copy-start.10
  104.0 1.2 %copy-start.9 = (f32[512,512]{1,0:T(8,128)S(1)}, f32[512,512]{1,0:T(8,128)}, u32[]{:S(2)}) copy-start(f32[512,512]{1,0:T(8,128)} %copy-done.8) | copy-start | bytes 3145732
  105.2 1.2 %copy-start.11 = (f32[512,512]{1,0:T(8,128)S(1)}, f32[512,512]{1,0:T(8,128)}, u32[]{:S(2)}) copy-start(f32[512,512]{1,0:T(8,128)} %copy-done.10) | copy-start | bytes 3145732

commit v2 on v1

v2 whole, which is shorter than its diff:
```python
import jax
import jax.numpy as jnp
from jax import lax
from jax.experimental import pallas as pl
from jax.experimental.pallas import tpu as pltpu
from jax.sharding import PartitionSpec as P

HEAD_DIM = 128
HIDDEN_DIMENSION = 4096
EPS = 1e-06
SCALE = HEAD_DIM ** (-0.5)
TOK = 512
HEADS = 4
BLOCKS = 64
PER_HEAD = BLOCKS // HEADS
HALF = TOK // 2
FAR = -1e9

F32 = jnp.float32
BF16 = jnp.bfloat16

NN = (((1,), (0,)), ((), ()))
NT = (((1,), (1,)), ((), ()))
TN = (((0,), (0,)), ((), ()))


def mm(a, b, dims=NN):
    return lax.dot_general(a, b, dims, preferred_element_type=F32)


def head(h):
    return slice(h * HEAD_DIM, (h + 1) * HEAD_DIM)


def pieces(x):
    hi = x.astype(BF16).astype(F32)
    rest = x - hi
    mid = rest.astype(BF16).astype(F32)
    return hi, mid, rest - mid


def fetch(source, target, sems, base):
    copies = []
    for h in range(HEADS):
        copy = pltpu.make_async_copy(
            source.at[:, head(h)], target.at[:, head(h)], sems.at[base + h]
        )
        copy.start()
        copies.append(copy)
    return copies


def aux_tile(row):
    hi, mid, lo = pieces(row)
    at = lax.broadcasted_iota(jnp.int32, (8, HEAD_DIM), 0)
    return jnp.where(at == 0, hi, jnp.where(at == 1, mid, jnp.where(at == 2, lo, 0.0)))


def message(matrix, tile):
    data = matrix.reshape(PER_HEAD, 8, HEAD_DIM)
    aux = jnp.broadcast_to(tile[None], (PER_HEAD, 8, HEAD_DIM))
    return jnp.concatenate([data, aux], axis=1).astype(BF16)


def summary_kernel(
    retention_far, keys_far, values_far, out, cum_out, keys, values, sems, retention, retention_sem
):
    got_retention = pltpu.make_async_copy(retention_far, retention, retention_sem)
    got_retention.start()
    got_keys = fetch(keys_far, keys, sems, 0)
    got_values = fetch(values_far, values, sems, HEADS)
    got_retention.wait()
    rows = jnp.concatenate([retention[...], jnp.zeros((8 - HEADS, TOK), F32)], axis=0)
    parts = pieces(rows)
    stacked = jnp.concatenate(
        [p[:, c * 128 : (c + 1) * 128] for c in range(TOK // 128) for p in parts], axis=0
    ).astype(BF16)
    first = lax.broadcasted_iota(jnp.int32, (128, 128), 0)
    second = lax.broadcasted_iota(jnp.int32, (128, 128), 1)
    upper = jnp.where(first <= second, 1.0, 0.0).astype(BF16)
    sums = mm(stacked, upper)
    offset = jnp.zeros((8, 1), F32)
    chunks = []
    for c in range(TOK // 128):
        own = sums[24 * c : 24 * c + 8] + sums[24 * c + 8 : 24 * c + 16] + sums[24 * c + 16 : 24 * c + 24]
        own = own + offset
        offset = own[:, 127:128]
        chunks.append(own)
    cum = jnp.concatenate(chunks, axis=1)
    cum_out[...] = cum
    tail = jnp.exp(offset - cum)
    decay = jnp.broadcast_to(jnp.exp(offset), (8, HEAD_DIM))
    for h in range(HEADS):
        got_keys[h].wait()
        turned = keys[:, head(h)].T
        key_decayed = (turned.astype(F32) * tail[h : h + 1]).astype(BF16)
        got_values[h].wait()
        out[h * PER_HEAD : (h + 1) * PER_HEAD] = message(
            mm(key_decayed, values[:, head(h)]), aux_tile(decay[h : h + 1])
        )


def decay_rows(aux):
    return jnp.broadcast_to(aux[0:1] + aux[1:2] + aux[2:3], (8, HEAD_DIM))


def forward_scan_kernel(arrived, out):
    state = jnp.zeros((8, HEAD_DIM), F32)
    for pair in range(BLOCKS // 2):
        both = []
        for b in (2 * pair, 2 * pair + 1):
            both.append(state)
            got = arrived[b].astype(F32)
            state = decay_rows(got[8:16]) * state + got[0:8]
        out[16 * pair : 16 * pair + 16] = jnp.concatenate(both, axis=0).astype(BF16)


def backward_scan_kernel(arrived, decays, out):
    state = jnp.zeros((8, HEAD_DIM), F32)
    for pair in reversed(range(BLOCKS // 2)):
        both = []
        for b in (2 * pair + 1, 2 * pair):
            both.append(state)
            state = decay_rows(decays[b].astype(F32)[8:16]) * state + arrived[b].astype(F32)[0:8]
        out[16 * pair : 16 * pair + 16] = jnp.concatenate(both[::-1], axis=0).astype(BF16)


def block_decay(cum, columns, h, i):
    rows, width = slice(i * HALF, (i + 1) * HALF), (i + 1) * HALF
    gap = columns[rows, h : h + 1] - cum[h : h + 1, 0:width]
    t = lax.broadcasted_iota(jnp.int32, (HALF, width), 0) + i * HALF
    s = lax.broadcasted_iota(jnp.int32, (HALF, width), 1)
    return jnp.exp(jnp.where(s <= t, gap, FAR))


def local_kernel(
    queries, keys_far, values_far, target, cum, gain, weight,
    local, turned, columns, rows_out, keys, values, sems,
):
    got_keys = fetch(keys_far, keys, sems, 0)
    got_values = fetch(values_far, values, sems, HEADS)
    total = cum[:, TOK - 1 : TOK]
    start = jnp.exp(cum[...]) * SCALE
    tail = jnp.exp(total - cum[...])
    side = jnp.concatenate([cum[...], start, tail, jnp.zeros((104, TOK), F32)], axis=0).T
    columns[...] = side
    square = jnp.zeros((TOK, HEAD_DIM), F32)
    for h in range(HEADS):
        x = target[:, head(h)].astype(F32)
        square = square + x * x
        got_keys[h].wait()
        got_values[h].wait()
        q, k, v = queries[:, head(h)], keys[:, head(h)], values[:, head(h)]
        turned[head(h), :] = (q.T.astype(F32) * start[h : h + 1]).astype(BF16)
        for i in range(2):
            rows, width = slice(i * HALF, (i + 1) * HALF), (i + 1) * HALF
            scores = mm(q[rows], k[0:width], NT)
            p = (scores * SCALE * block_decay(cum, side, h, i)).astype(BF16)
            local[rows, head(h)] = mm(p, v[0:width])
    rows_out[...] = jnp.concatenate(
        [gain[...], weight[...], jnp.sum(square.T, axis=0, keepdims=True), jnp.zeros((5, TOK), F32)],
        axis=0,
    )


def output_kernel(queries, states, local, columns, target, rows, attn, sums):
    square = jnp.zeros((TOK, HEAD_DIM), F32)
    gain_square = square
    cross = square
    for h in range(HEADS):
        carried = mm(queries[:, head(h)], states[head(h), :])
        o = local[:, head(h)] + columns[:, 8 + h : 9 + h] * carried
        attn[:, head(h)] = o
        gained = rows[0:1, head(h)] * o
        square = square + o * o
        gain_square = gain_square + gained * gained
        cross = cross + gained * target[:, head(h)].astype(F32)
    four = jnp.concatenate(
        [jnp.sum(a.T, axis=0, keepdims=True) for a in (square, gain_square, cross)]
        + [rows[2:3]],
        axis=0,
    )
    for d in range(8):
        sums[d] = four


def gradient_kernel(sums, attn, target, rows, turned, out, grad_out):
    weight = rows[1:2]
    four = jnp.sum(sums[...], axis=0)
    mean_square = four[0:1] / HIDDEN_DIMENSION + EPS
    inverse = 1.0 / jnp.sqrt(mean_square)
    pred_square = four[1:2] / mean_square
    pred_cross = four[2:3] * inverse
    inner = weight * (pred_square - pred_cross)
    a = weight / mean_square
    b = weight * inverse
    c = inner / (HIDDEN_DIMENSION * mean_square)
    side = jnp.concatenate([a, b, c, jnp.zeros((125, TOK), F32)], axis=0).T
    a, b, c = side[:, 0:1], side[:, 1:2], side[:, 2:3]
    gains, backs = [], []
    for h in range(HEADS):
        o, x, g = attn[:, head(h)], target[:, head(h)].astype(F32), rows[0:1, head(h)]
        error = a * (g * o) - b * x
        gains.append(jnp.sum(error * o, axis=0, keepdims=True))
        d = (error * g - c * o).astype(BF16)
        grad_out[:, head(h)] = d
        backs.append(mm(turned[head(h), :], d))
    gains = jnp.concatenate(gains, axis=0)
    high = gains.astype(BF16).astype(F32)
    tile = jnp.concatenate([high, gains - high], axis=0)
    for h in range(HEADS):
        out[h * PER_HEAD : (h + 1) * PER_HEAD] = message(backs[h], tile)


def local_gradient_kernel(
    grad_out, queries, keys_far, values_far, states, cum, columns, sums, arrived,
    grad_q, local_k, local_v, payoff, gain_out, keys, values, sems,
):
    got_keys = fetch(keys_far, keys, sems, 0)
    got_values = fetch(values_far, values, sems, HEADS)
    four = jnp.sum(sums[...], axis=0)
    mean_square = four[0:1] / HIDDEN_DIMENSION + EPS
    pred_square = four[1:2] / mean_square
    pred_cross = four[2:3] / jnp.sqrt(mean_square)
    payoff[...] = (pred_square - 2.0 * pred_cross + four[3:4]) / HIDDEN_DIMENSION
    gains = jnp.zeros((8, HEAD_DIM), F32)
    for b in range(BLOCKS):
        gains = gains + arrived[b].astype(F32)[8:16]
    gain_out[...] = (gains[0:HEADS] + gains[HEADS : 2 * HEADS]) / (BLOCKS * TOK)
    for h in range(HEADS):
        got_keys[h].wait()
        got_values[h].wait()
        q, k, v, d = queries[:, head(h)], keys[:, head(h)], values[:, head(h)], grad_out[:, head(h)]
        carried = columns[:, 8 + h : 9 + h] * mm(d, states[head(h), :], NT)
        parts, probs = [], []
        for i in range(2):
            rows, width = slice(i * HALF, (i + 1) * HALF), (i + 1) * HALF
            decay = SCALE * block_decay(cum, columns, h, i)
            probs.append((mm(q[rows], k[0:width], NT) * decay).astype(BF16))
            gp = (mm(d[rows], v[0:width], NT) * decay).astype(BF16)
            parts.append(gp)
            grad_q[rows, head(h)] = (mm(gp, k[0:width]) + carried[rows]).astype(BF16)
        for side, near, far in ((local_k, parts, q), (local_v, probs, d)):
            early = jnp.concatenate([near[0], near[1][:, 0:HALF]], axis=0)
            side[0:HALF, head(h)] = mm(early, far, TN).astype(BF16)
            side[HALF:TOK, head(h)] = mm(near[1][:, HALF:TOK], far[HALF:TOK], TN).astype(BF16)


def final_kernel(
    states, keys, values, local_k, local_v, columns, grad_k_far, grad_v_far, grad_k, grad_v, sems
):
    copies = []
    for h in range(HEADS):
        state = states[head(h), :]
        tail = columns[:, 16 + h : 17 + h]
        for i, (near, far, local, moved) in enumerate(
            (
                (grad_k, grad_k_far, local_k, mm(values[:, head(h)], state, NT)),
                (grad_v, grad_v_far, local_v, mm(keys[:, head(h)], state)),
            )
        ):
            near[:, head(h)] = (local[:, head(h)].astype(F32) + tail * moved).astype(BF16)
            copy = pltpu.make_async_copy(
                near.at[:, head(h)], far.at[:, head(h)], sems.at[2 * h + i]
            )
            copy.start()
            copies.append(copy)
    for copy in copies:
        copy.wait()


NEAR = pl.BlockSpec(memory_space=pltpu.VMEM)
FAR_AWAY = pl.BlockSpec(memory_space=pltpu.HBM)


def call(kernel, outs, args, flops, name, far=(), far_outs=(), pairs=False, more=()):
    moved = sum(a.size * a.dtype.itemsize for a in args)
    moved += sum(o.size * o.dtype.itemsize for o in outs)
    scratch = []
    if pairs:
        scratch = [pltpu.VMEM((TOK, TOK), BF16)] * 2 + [pltpu.SemaphoreType.DMA((2 * HEADS,))]
    return pl.pallas_call(
        kernel,
        out_shape=outs,
        in_specs=[FAR_AWAY if i in far else NEAR for i in range(len(args))],
        out_specs=[FAR_AWAY if i in far_outs else NEAR for i in range(len(outs))],
        scratch_shapes=[*scratch, *more],
        compiler_params=pltpu.CompilerParams(vmem_limit_bytes=32 * 2**20),
        cost_estimate=pl.CostEstimate(flops=flops, bytes_accessed=moved, transcendentals=0),
        name=name,
    )(*(pltpu.with_memory_space_constraint(a, pltpu.HBM) if i in far else a for i, a in enumerate(args)))


def shape(dims, kind):
    return jax.ShapeDtypeStruct(dims, kind)


def exchange(x, axis):
    return lax.all_to_all(x, axis, 0, 0, tiled=True)


def local_part(queries, keys, values, retention, target, gain, weight):
    wide = TOK * TOK * HEAD_DIM * 2 * HEADS
    narrow = TOK * HEAD_DIM * HEAD_DIM * 2 * HEADS
    gain = gain.reshape(1, -1)
    weight = weight.reshape(1, -1)
    slices = shape((BLOCKS, 16, HEAD_DIM), BF16)
    full32 = shape((TOK, TOK), F32)
    full16 = shape((TOK, TOK), BF16)
    row = shape((1, TOK), F32)

    sent, cum = call(
        summary_kernel,
        [slices, shape((8, TOK), F32)],
        [retention, keys, values],
        narrow,
        "summary",
        far=(0, 1, 2),
        pairs=True,
        more=[pltpu.VMEM((HEADS, TOK), F32), pltpu.SemaphoreType.DMA],
    )
    arrived = exchange(sent, "ctx")
    local, turned, columns, rows = call(
        local_kernel,
        [full32, full16, shape((TOK, 128), F32), shape((8, TOK), F32)],
        [queries, keys, values, target, cum, gain, weight],
        2 * wide,
        "local",
        far=(1, 2),
        pairs=True,
    )
    back = shape((TOK, HEAD_DIM), BF16)
    [states] = call(forward_scan_kernel, [back], [arrived], 1000, "forward_scan")
    states = exchange(states.reshape(BLOCKS, 8, HEAD_DIM), "ctx").reshape(TOK, HEAD_DIM)
    attn, sums = call(
        output_kernel,
        [full32, shape((8, 4, TOK), F32)],
        [queries, states, local, columns, target, rows],
        narrow,
        "output",
    )
    sums = exchange(sums, "head")
    sent, grad_out = call(
        gradient_kernel, [slices, full16], [sums, attn, target, rows, turned], narrow, "gradient"
    )
    arrived_back = exchange(sent, "ctx")
    grad_q, local_k, local_v, payoff, gain_out = call(
        local_gradient_kernel,
        [full16, full16, full16, row, shape((HEADS, HEAD_DIM), F32)],
        [grad_out, queries, keys, values, states, cum, columns, sums, arrived_back],
        6 * wide,
        "local_gradient",
        far=(2, 3),
        pairs=True,
    )
    [later] = call(backward_scan_kernel, [back], [arrived_back, arrived], 1000, "backward_scan")
    later = exchange(later.reshape(BLOCKS, 8, HEAD_DIM), "ctx").reshape(TOK, HEAD_DIM)
    grad_k, grad_v = call(
        final_kernel,
        [full16, full16],
        [later, keys, values, local_k, local_v, columns],
        2 * narrow,
        "final",
        far_outs=(0, 1),
        pairs=True,
    )
    return payoff.reshape(-1), grad_q, grad_k, grad_v, gain_out.reshape(-1)


def solution(mesh):
    placed = (
        P("ctx", "head"),
        P("ctx", "head"),
        P("ctx", "head"),
        P("head", "ctx"),
        P("ctx", "head"),
        P("head"),
        P("ctx"),
    )
    return jax.shard_map(
        local_part,
        mesh=mesh,
        in_specs=placed,
        out_specs=(P("ctx"), P("ctx", "head"), P("ctx", "head"), P("ctx", "head"), P("head")),
        check_vma=False,
    )
```

time: 110 us -> 103 us (0.936); the launches traced: 108 us -> 102 us
  local copies, waits for them, and re-layouts: 13.1 us -> 2.52 us
  Pallas kernels: 11.1 us -> 16.4 us
    unnamed x38 -> x20, local copies, waits for them, and re-layouts: 13.1 us -> 2.52 us
    pallas_call x8, Pallas kernels: 11.1 us -> 16.4 us  [call(): pl.pallas_call(kernel, out_shape=outs, in_specs=[FAR_AWAY if i in far els...]
  transfers between devices with their start and end apart: 2 -> 2, of which waited for: 2 -> 2; matrix products, arithmetic and copies ran while one was open for 0% -> 0% of each run, Pallas kernels for 5% -> 9%
where the time goes in v2:
time: 103 us; the launch traced here: 102 us
  blocking collectives  58.9 us (57%)
  Pallas kernels  16.4 us (16%)
  starting transfers between devices  12.2 us (12%)
  waiting for transfers between devices  11.2 us (11%)
  local copies, waits for them, and re-layouts  2.52 us (2%)
    all_to_all x3, blocking collectives, exchange(): return lax.all_to_all(x, axis, 0, 0, tiled=True)  58.9 us
    pallas_call x8, Pallas kernels, call(): pl.pallas_call(kernel, out_shape=outs, in_specs=[FAR_AWAY if i in far els...  16.4 us
    all_to_all x2, starting transfers between devices, exchange(): return lax.all_to_all(x, axis, 0, 0, tiled=True)  12.2 us
    all_to_all x2, waiting for transfers between devices, exchange(): return lax.all_to_all(x, axis, 0, 0, tiled=True)  11.2 us
    unnamed x20, local copies, waits for them, and re-layouts  2.52 us
  transfers between devices with their start and end apart: 2, of which 2 were waited for; matrix products, arithmetic and copies ran while one was open for 0% of the time, Pallas kernels for 9%

profile of v2, /device:TPU:1, one launch (start us, length us, event | category | flops | bytes accessed | tf_op | source)
XLA Modules:
  0.0 102.1 jit_solution(6130985957645858434)
XLA Ops:
  0.6 2.7 %summary.1 = (bf16[64,16,128]{2,1,0:T(8,128)(2,1)S(1)}, f32[8,512]{1,0:T(8,128)S(1)}) custom-call(f32[4,512]{1,0:T(4,128)} %retention_far.1, bf16[512,512]{1,0:T(8,128)(2,1)} %keys.1, bf16[512,512]{1,0:T(8,128)(2,1)} %values.1), custom_call_target="tpu_custom_call" | custom-call | flops 67108864 | bytes 1335296 | tf_op jit(solution)/shard_map/summary/pallas_call | solution.py:282
  3.3 0.0 copy-start.2
  3.3 0.0 copy-start.3
  3.3 29.6 %all_to_all.25.arrived.decays = bf16[64,16,128]{2,1,0:T(8,128)(2,1)S(1)} all-to-all(bf16[64,16,128]{2,1,0:T(8,128)(2,1)S(1)} %get-tuple-element.22), channel_id=1, replica_groups=mesh['ctx'=64,'head'=8] {'ctx'}, dimensions={0} | all-to-all | bytes 524288 | tf_op jit(solution)/shard_map/all_to_all | solution.py:299
  33.0 0.8 forward_scan.1
  33.8 5.9 %all-to-all-start.1 = ((bf16[64,8,128]{2,1,0:T(8,128)(2,1)}), bf16[64,8,128]{2,1,0:T(8,128)(2,1)S(1)}, u32[]{:S(2)}, u32[]{:S(2)}) async-start(bf16[64,8,128]{2,1,0:T(8,128)(2,1)} %bitcast), calls=%async_computation.1 | async-start | bytes 262144 | tf_op jit(solution)/shard_map/all_to_all | solution.py:299
  39.6 0.0 copy-start.7
  39.6 0.0 copy-start.6
  39.7 0.0 copy-done.2
  39.7 0.0 copy-done.3
  39.7 0.6 copy-done.7
  40.3 0.0 copy-done.6
  40.3 3.5 %local.1 = (f32[512,512]{1,0:T(8,128)S(1)}, bf16[512,512]{1,0:T(8,128)(2,1)S(1)}, f32[512,128]{1,0:T(8,128)S(1)}, f32[8,512]{1,0:T(8,128)S(1)}) custom-call(bf16[512,512]{1,0:T(8,128)(2,1)S(1)} %copy-done.3, bf16[512,512]{1,0:T(8,128)(2,1)} %keys.1, bf16[512,512]{1,0:T(8,128)(2,1)} %values.1, bf16[512,512]{1,0:T(8,128)(2,1)S(1)} %copy-done.2, ...), custom_call_target="tpu_custom_call" | custom-call | flops 536870912 | bytes 3969024 | tf_op jit(solution)/shard_map/local/pallas_call | solution.py:282
  43.8 0.0 copy-start.4
  43.8 0.8 copy-done.4
  44.6 6.5 %all-to-all-done.1 = bf16[64,8,128]{2,1,0:T(8,128)(2,1)S(1)} async-done(((bf16[64,8,128]{2,1,0:T(8,128)(2,1)}), bf16[64,8,128]{2,1,0:T(8,128)(2,1)S(1)}, u32[]{:S(2)}, u32[]{:S(2)}) %all-to-all-start.1) | async-done | bytes 131104 | tf_op jit(solution)/shard_map/all_to_all | solution.py:299
  51.1 0.0 copy-start.5
  51.1 0.8 output.1
  51.9 12.3 %all_to_all.26.sums = f32[8,4,512]{2,1,0:T(4,128)S(1)} all-to-all(f32[8,4,512]{2,1,0:T(4,128)S(1)} %get-tuple-element.27), channel_id=1, replica_groups=mesh['ctx'=64,'head'=8] {'head'}, dimensions={0} | all-to-all | bytes 131072 | tf_op jit(solution)/shard_map/all_to_all | solution.py:299
  64.2 0.0 copy-done.5
  64.2 0.9 gradient.1
  65.2 0.0 copy-start.8
  65.2 16.9 %all_to_all.27.arrived = bf16[64,16,128]{2,1,0:T(8,128)(2,1)S(1)} all-to-all(bf16[64,16,128]{2,1,0:T(8,128)(2,1)S(1)} %get-tuple-element.31), channel_id=1, replica_groups=mesh['ctx'=64,'head'=8] {'ctx'}, dimensions={0} | all-to-all | bytes 524288 | tf_op jit(solution)/shard_map/all_to_all | solution.py:299
  82.1 0.8 backward_scan.1
  82.9 0.0 copy-done.8
  82.9 6.3 %all-to-all-start.4 = ((bf16[64,8,128]{2,1,0:T(8,128)(2,1)}), bf16[64,8,128]{2,1,0:T(8,128)(2,1)S(1)}, u32[]{:S(2)}, u32[]{:S(2)}) async-start(bf16[64,8,128]{2,1,0:T(8,128)(2,1)} %bitcast.5), calls=%async_computation.4 | async-start | bytes 262144 | tf_op jit(solution)/shard_map/all_to_all | solution.py:299
  89.2 0.0 copy-start.9
  89.2 1.0 %copy-done.9 = bf16[512,512]{1,0:T(8,128)(2,1)S(1)} copy-done((bf16[512,512]{1,0:T(8,128)(2,1)S(1)}, bf16[512,512]{1,0:T(8,128)(2,1)}, u32[]{:S(2)}) %copy-start.9) | copy-done | bytes 524312
  90.3 0.0 copy-start
  90.3 0.0 copy-start.1
  90.3 5.7 %local_gradient.1 = (bf16[512,512]{1,0:T(8,128)(2,1)}, bf16[512,512]{1,0:T(8,128)(2,1)S(1)}, bf16[512,512]{1,0:T(8,128)(2,1)S(1)}, f32[1,512]{1,0:T(1,128)}, f32[4,128]{1,0:T(4,128)}) custom-call(bf16[512,512]{1,0:T(8,128)(2,1)S(1)} %copy-done.9, bf16[512,512]{1,0:T(8,128)(2,1)S(1)} %copy-done.3, bf16[512,512]{1,0:T(8,128)(2,1)} %keys.1, ...), custom_call_target="tpu_custom_call" | custom-call | flops 1610612736 | bytes 4411392 | tf_op jit(solution)/shard_map/local_gradient/pallas_call | solution.py:282
  96.0 4.6 %all-to-all-done.4 = bf16[64,8,128]{2,1,0:T(8,128)(2,1)S(1)} async-done(((bf16[64,8,128]{2,1,0:T(8,128)(2,1)}), bf16[64,8,128]{2,1,0:T(8,128)(2,1)S(1)}, u32[]{:S(2)}, u32[]{:S(2)}) %all-to-all-start.4) | async-done | bytes 131104 | tf_op jit(solution)/shard_map/all_to_all | solution.py:299
  100.6 0.0 copy-done
  100.6 0.0 copy-done.1
  100.6 1.3 %final.1 = (bf16[512,512]{1,0:T(8,128)(2,1)}, bf16[512,512]{1,0:T(8,128)(2,1)}) custom-call(bf16[512,128]{1,0:T(8,128)(2,1)S(1)} %bitcast.10, bf16[512,512]{1,0:T(8,128)(2,1)S(1)} %copy-done, bf16[512,512]{1,0:T(8,128)(2,1)S(1)} %copy-done.1, bf16[512,512]{1,0:T(8,128)(2,1)S(1)} %get-tuple-element.34.local_k, ...), custom_call_target="tpu_custom_call" | custom-call | flops 134217728 | bytes 3538944 | tf_op jit(solution)/shard_map/final/pallas_call | solution.py:282
Async XLA Ops:
  3.3 36.3 %copy-start.2 = (bf16[512,512]{1,0:T(8,128)(2,1)S(1)}, bf16[512,512]{1,0:T(8,128)(2,1)}, u32[]{:S(2)}) copy-start(bf16[512,512]{1,0:T(8,128)(2,1)} %target.5) | copy-start | bytes 1572868
  3.3 36.3 %copy-start.3 = (bf16[512,512]{1,0:T(8,128)(2,1)S(1)}, bf16[512,512]{1,0:T(8,128)(2,1)}, u32[]{:S(2)}) copy-start(bf16[512,512]{1,0:T(8,128)(2,1)} %queries.5) | copy-start | bytes 1572868
  33.8 17.4 %all-to-all-start.1 = ((bf16[64,8,128]{2,1,0:T(8,128)(2,1)}), bf16[64,8,128]{2,1,0:T(8,128)(2,1)S(1)}, u32[]{:S(2)}, u32[]{:S(2)}) async-start(bf16[64,8,128]{2,1,0:T(8,128)(2,1)} %bitcast), calls=%async_computation.1 | async-start | bytes 262144 | tf_op jit(solution)/shard_map/all_to_all | solution.py:299
  39.6 0.7 copy-start.7
  39.6 0.7 copy-start.6
  43.8 0.8 copy-start.4
  51.1 13.1 %copy-start.5 = (bf16[512,512]{1,0:T(8,128)(2,1)S(1)}, bf16[512,512]{1,0:T(8,128)(2,1)}, u32[]{:S(2)}) copy-start(bf16[512,512]{1,0:T(8,128)(2,1)} %copy-done.4) | copy-start | bytes 1572868
  65.2 17.7 %copy-start.8 = (bf16[512,512]{1,0:T(8,128)(2,1)}, bf16[512,512]{1,0:T(8,128)(2,1)S(1)}, u32[]{:S(2)}) copy-start(bf16[512,512]{1,0:T(8,128)(2,1)S(1)} %get-tuple-element.30.grad_out) | copy-start | bytes 1572868
  82.9 17.7 %all-to-all-start.4 = ((bf16[64,8,128]{2,1,0:T(8,128)(2,1)}), bf16[64,8,128]{2,1,0:T(8,128)(2,1)S(1)}, u32[]{:S(2)}, u32[]{:S(2)}) async-start(bf16[64,8,128]{2,1,0:T(8,128)(2,1)} %bitcast.5), calls=%async_computation.4 | async-start | bytes 262144 | tf_op jit(solution)/shard_map/all_to_all | solution.py:299
  89.2 1.0 %copy-start.9 = (bf16[512,512]{1,0:T(8,128)(2,1)S(1)}, bf16[512,512]{1,0:T(8,128)(2,1)}, u32[]{:S(2)}) copy-start(bf16[512,512]{1,0:T(8,128)(2,1)} %copy-done.8) | copy-start | bytes 1572868
  90.3 10.4 %copy-start = (bf16[512,512]{1,0:T(8,128)(2,1)S(1)}, bf16[512,512]{1,0:T(8,128)(2,1)}, u32[]{:S(2)}) copy-start(bf16[512,512]{1,0:T(8,128)(2,1)} %keys.1) | copy-start | bytes 1572868
  90.3 10.4 %copy-start.1 = (bf16[512,512]{1,0:T(8,128)(2,1)S(1)}, bf16[512,512]{1,0:T(8,128)(2,1)}, u32[]{:S(2)}) copy-start(bf16[512,512]{1,0:T(8,128)(2,1)} %values.1) | copy-start | bytes 1572868

commit v3 on v2

v3 whole, which is shorter than its diff:
```python
import math

import jax
import jax.numpy as jnp
from jax import lax
from jax.experimental import pallas as pl
from jax.experimental.pallas import tpu as pltpu
from jax.sharding import PartitionSpec as P

HEAD_DIM = 128
HIDDEN_DIMENSION = 4096
EPS = 1e-06
SCALE = HEAD_DIM ** (-0.5)
TOK = 512
HEADS = 4
BLOCKS = 64
PER_HEAD = BLOCKS // HEADS
HALF = TOK // 2
FAR = -1e9
LOG2E = math.log2(math.e)
LOG2_SCALE = math.log2(SCALE)

F32 = jnp.float32
BF16 = jnp.bfloat16

NN = (((1,), (0,)), ((), ()))
NT = (((1,), (1,)), ((), ()))
TN = (((0,), (0,)), ((), ()))


def mm(a, b, dims=NN):
    return lax.dot_general(a, b, dims, preferred_element_type=F32)


def head(h):
    return slice(h * HEAD_DIM, (h + 1) * HEAD_DIM)


def pieces(x):
    hi = x.astype(BF16).astype(F32)
    rest = x - hi
    mid = rest.astype(BF16).astype(F32)
    return hi, mid, rest - mid


def copy(source, target, sem):
    moving = pltpu.make_async_copy(source, target, sem)
    moving.start()
    return moving


def aux_tile(row):
    hi, mid, lo = pieces(row)
    at = lax.broadcasted_iota(jnp.int32, (8, HEAD_DIM), 0)
    return jnp.where(at == 0, hi, jnp.where(at == 1, mid, jnp.where(at == 2, lo, 0.0)))


def message(matrix, tile):
    data = matrix.reshape(PER_HEAD, 8, HEAD_DIM)
    aux = jnp.broadcast_to(tile[None], (PER_HEAD, 8, HEAD_DIM))
    return jnp.concatenate([data, aux], axis=1).astype(BF16)


def summary_kernel(
    retention_far, keys_far, values_far, gain_far, weight_far,
    out, cum_out, keys, values, gain, weight, retention, sems,
):
    got_retention = copy(retention_far, retention, sems.at[0])
    got_keys = copy(keys_far, keys, sems.at[1])
    got_values = copy(values_far, values, sems.at[2])
    got_gain = copy(gain_far, gain, sems.at[3])
    got_weight = copy(weight_far, weight, sems.at[4])
    got_retention.wait()
    rows = jnp.concatenate([retention[...], jnp.zeros((8 - HEADS, TOK), F32)], axis=0)
    parts = pieces(rows)
    stacked = jnp.concatenate(
        [p[:, c * 128 : (c + 1) * 128] for c in range(TOK // 128) for p in parts], axis=0
    ).astype(BF16)
    first = lax.broadcasted_iota(jnp.int32, (128, 128), 0)
    second = lax.broadcasted_iota(jnp.int32, (128, 128), 1)
    upper = jnp.where(first <= second, 1.0, 0.0).astype(BF16)
    sums = mm(stacked, upper)
    offset = jnp.zeros((8, 1), F32)
    chunks = []
    for c in range(TOK // 128):
        own = sums[24 * c : 24 * c + 8] + sums[24 * c + 8 : 24 * c + 16] + sums[24 * c + 16 : 24 * c + 24]
        own = own + offset
        offset = own[:, 127:128]
        chunks.append(own)
    cum = jnp.concatenate(chunks, axis=1)
    cum_out[...] = cum
    tail = jnp.exp(offset - cum)
    decay = jnp.broadcast_to(jnp.exp(offset), (8, HEAD_DIM))
    got_keys.wait()
    got_values.wait()
    for h in range(HEADS):
        turned = keys[:, head(h)].T
        key_decayed = (turned.astype(F32) * tail[h : h + 1]).astype(BF16)
        out[h * PER_HEAD : (h + 1) * PER_HEAD] = message(
            mm(key_decayed, values[:, head(h)]), aux_tile(decay[h : h + 1])
        )
    got_gain.wait()
    got_weight.wait()


def decay_rows(aux):
    return jnp.broadcast_to(aux[0:1] + aux[1:2] + aux[2:3], (8, HEAD_DIM))


def forward_scan(arrived, out):
    state = jnp.zeros((8, HEAD_DIM), F32)
    for pair in range(BLOCKS // 2):
        both = []
        for b in (2 * pair, 2 * pair + 1):
            both.append(state)
            got = arrived[b].astype(F32)
            state = decay_rows(got[8:16]) * state + got[0:8]
        out[16 * pair : 16 * pair + 16] = jnp.concatenate(both, axis=0).astype(BF16)


def backward_scan_kernel(arrived, decays, out):
    state = jnp.zeros((8, HEAD_DIM), F32)
    for pair in reversed(range(BLOCKS // 2)):
        both = []
        for b in (2 * pair + 1, 2 * pair):
            both.append(state)
            state = decay_rows(decays[b].astype(F32)[8:16]) * state + arrived[b].astype(F32)[0:8]
        out[16 * pair : 16 * pair + 16] = jnp.concatenate(both[::-1], axis=0).astype(BF16)


def block_decay(logs, columns, h, i):
    rows, width = slice(i * HALF, (i + 1) * HALF), (i + 1) * HALF
    gap = columns[rows, h : h + 1] - logs[h : h + 1, 0:width]
    t = lax.broadcasted_iota(jnp.int32, (HALF, HALF), 0)
    s = lax.broadcasted_iota(jnp.int32, (HALF, HALF), 1)
    last = jnp.where(s <= t, gap[:, i * HALF :], FAR)
    return jnp.exp2(last if i == 0 else jnp.concatenate([gap[:, 0:HALF], last], axis=1))


def local_kernel(
    arrived, queries, keys, values, target, cum, states, local, turned, columns, target_square
):
    forward_scan(arrived, states)
    total = cum[:, TOK - 1 : TOK]
    start = jnp.exp(cum[...]) * SCALE
    tail = jnp.exp(total - cum[...])
    logs = cum[...] * LOG2E
    side = jnp.concatenate([logs + LOG2_SCALE, start, tail, jnp.zeros((104, TOK), F32)], axis=0).T
    columns[...] = side
    square = jnp.zeros((TOK, HEAD_DIM), F32)
    for h in range(HEADS):
        x = target[:, head(h)].astype(F32)
        square = square + x * x
        q, k, v = queries[:, head(h)], keys[:, head(h)], values[:, head(h)]
        turned[head(h), :] = (q.T.astype(F32) * start[h : h + 1]).astype(BF16)
        for i in range(2):
            rows, width = slice(i * HALF, (i + 1) * HALF), (i + 1) * HALF
            p = (mm(q[rows], k[0:width], NT) * block_decay(logs, side, h, i)).astype(BF16)
            local[rows, head(h)] = mm(p, v[0:width])
    target_square[...] = jnp.sum(square.T, axis=0, keepdims=True)


def output_kernel(queries, states, local, columns, target, gain, target_square, attn, sums):
    square = jnp.zeros((TOK, HEAD_DIM), F32)
    gain_square = square
    cross = square
    for h in range(HEADS):
        carried = mm(queries[:, head(h)], states[head(h), :])
        o = local[:, head(h)] + columns[:, 8 + h : 9 + h] * carried
        attn[:, head(h)] = o
        gained = gain[:, head(h)] * o
        square = square + o * o
        gain_square = gain_square + gained * gained
        cross = cross + gained * target[:, head(h)].astype(F32)
    four = jnp.concatenate(
        [jnp.sum(a.T, axis=0, keepdims=True) for a in (square, gain_square, cross)]
        + [target_square[...]],
        axis=0,
    )
    for d in range(8):
        sums[d] = four


def gradient_kernel(sums, attn, target, gain, weight, turned, out, grad_out):
    four = jnp.sum(sums[...], axis=0)
    mean_square = four[0:1] / HIDDEN_DIMENSION + EPS
    inverse = 1.0 / jnp.sqrt(mean_square)
    pred_square = four[1:2] / mean_square
    pred_cross = four[2:3] * inverse
    inner = weight[...] * (pred_square - pred_cross)
    a = weight[...] / mean_square
    b = weight[...] * inverse
    c = inner / (HIDDEN_DIMENSION * mean_square)
    side = jnp.concatenate([a, b, c, jnp.zeros((125, TOK), F32)], axis=0).T
    a, b, c = side[:, 0:1], side[:, 1:2], side[:, 2:3]
    gains, backs = [], []
    for h in range(HEADS):
        o, x, g = attn[:, head(h)], target[:, head(h)].astype(F32), gain[:, head(h)]
        error = a * (g * o) - b * x
        gains.append(jnp.sum(error * o, axis=0, keepdims=True))
        d = (error * g - c * o).astype(BF16)
        grad_out[:, head(h)] = d
        backs.append(mm(turned[head(h), :], d))
    gains = jnp.concatenate(gains, axis=0)
    high = gains.astype(BF16).astype(F32)
    tile = jnp.concatenate([high, gains - high], axis=0)
    for h in range(HEADS):
        out[h * PER_HEAD : (h + 1) * PER_HEAD] = message(backs[h], tile)


def local_gradient_kernel(
    grad_out, queries, keys_far, values_far, states, cum, columns, sums, arrived,
    grad_q, local_k, local_v, payoff, gain_out, keys, values, sems,
):
    got_keys = copy(keys_far, keys, sems.at[0])
    got_values = copy(values_far, values, sems.at[1])
    logs = cum[...] * LOG2E
    four = jnp.sum(sums[...], axis=0)
    mean_square = four[0:1] / HIDDEN_DIMENSION + EPS
    pred_square = four[1:2] / mean_square
    pred_cross = four[2:3] / jnp.sqrt(mean_square)
    payoff[...] = (pred_square - 2.0 * pred_cross + four[3:4]) / HIDDEN_DIMENSION
    gains = jnp.zeros((8, HEAD_DIM), F32)
    for b in range(BLOCKS):
        gains = gains + arrived[b].astype(F32)[8:16]
    gain_out[...] = (gains[0:HEADS] + gains[HEADS : 2 * HEADS]) / (BLOCKS * TOK)
    got_keys.wait()
    got_values.wait()
    for h in range(HEADS):
        q, k, v, d = queries[:, head(h)], keys[:, head(h)], values[:, head(h)], grad_out[:, head(h)]
        carried = columns[:, 8 + h : 9 + h] * mm(d, states[head(h), :], NT)
        parts, probs = [], []
        for i in range(2):
            rows, width = slice(i * HALF, (i + 1) * HALF), (i + 1) * HALF
            decay = block_decay(logs, columns, h, i)
            probs.append((mm(q[rows], k[0:width], NT) * decay).astype(BF16))
            gp = (mm(d[rows], v[0:width], NT) * decay).astype(BF16)
            parts.append(gp)
            grad_q[rows, head(h)] = (mm(gp, k[0:width]) + carried[rows]).astype(BF16)
        for side, near, far in ((local_k, parts, q), (local_v, probs, d)):
            early = jnp.concatenate([near[0], near[1][:, 0:HALF]], axis=0)
            side[0:HALF, head(h)] = mm(early, far, TN).astype(BF16)
            side[HALF:TOK, head(h)] = mm(near[1][:, HALF:TOK], far[HALF:TOK], TN).astype(BF16)


def final_kernel(
    states, keys, values, local_k, local_v, columns, grad_k_far, grad_v_far, grad_k, grad_v, sems
):
    moving = []
    for h in range(HEADS):
        tail, state = columns[:, 16 + h : 17 + h], states[head(h), :]
        for near, far, local, side, dims in (
            (grad_k, grad_k_far, local_k, values, NT),
            (grad_v, grad_v_far, local_v, keys, NN),
        ):
            moved = tail * mm(side[:, head(h)], state, dims)
            near[:, head(h)] = (local[:, head(h)].astype(F32) + moved).astype(BF16)
            moving.append(copy(near.at[:, head(h)], far.at[:, head(h)], sems.at[len(moving)]))
    for one in moving:
        one.wait()


NEAR = pl.BlockSpec(memory_space=pltpu.VMEM)
FAR_AWAY = pl.BlockSpec(memory_space=pltpu.HBM)


def call(kernel, outs, args, flops, name, far=(), far_outs=(), scratch=()):
    moved = sum(a.size * a.dtype.itemsize for a in args)
    moved += sum(o.size * o.dtype.itemsize for o in outs)
    placed = [pltpu.with_memory_space_constraint(a, pltpu.HBM) if i in far else a for i, a in enumerate(args)]
    return pl.pallas_call(
        kernel,
        out_shape=outs,
        in_specs=[FAR_AWAY if i in far else NEAR for i in range(len(args))],
        out_specs=[FAR_AWAY if i in far_outs else NEAR for i in range(len(outs))],
        scratch_shapes=scratch,
        compiler_params=pltpu.CompilerParams(vmem_limit_bytes=32 * 2**20),
        cost_estimate=pl.CostEstimate(flops=flops, bytes_accessed=moved, transcendentals=0),
        name=name,
    )(*placed)


def shape(dims, kind):
    return jax.ShapeDtypeStruct(dims, kind)


def exchange(x, axis):
    return lax.all_to_all(x, axis, 0, 0, tiled=True)


def local_part(queries, keys, values, retention, target, gain, weight):
    wide = TOK * TOK * HEAD_DIM * 2 * HEADS
    narrow = TOK * HEAD_DIM * HEAD_DIM * 2 * HEADS
    gain = gain.reshape(1, -1)
    weight = weight.reshape(1, -1)
    slices = shape((BLOCKS, 16, HEAD_DIM), BF16)
    full32 = shape((TOK, TOK), F32)
    full16 = shape((TOK, TOK), BF16)
    row = shape((1, TOK), F32)

    pair = [pltpu.VMEM((TOK, TOK), BF16)] * 2 + [pltpu.SemaphoreType.DMA((2,))]
    sent, cum, near_keys, near_values, gain, weight = call(
        summary_kernel,
        [slices, shape((8, TOK), F32), full16, full16, row, row],
        [retention, keys, values, gain, weight],
        narrow,
        "summary",
        far=(0, 1, 2, 3, 4),
        scratch=[pltpu.VMEM((HEADS, TOK), F32), pltpu.SemaphoreType.DMA((5,))],
    )
    arrived = exchange(sent, "ctx")
    back = shape((TOK, HEAD_DIM), BF16)
    states, local, turned, columns, target_square = call(
        local_kernel,
        [back, full32, full16, shape((TOK, 128), F32), row],
        [arrived, queries, near_keys, near_values, target, cum],
        2 * wide,
        "local",
    )
    states = exchange(states.reshape(BLOCKS, 8, HEAD_DIM), "ctx").reshape(TOK, HEAD_DIM)
    attn, sums = call(
        output_kernel,
        [full32, shape((8, 4, TOK), F32)],
        [queries, states, local, columns, target, gain, target_square],
        narrow,
        "output",
    )
    sums = exchange(sums, "head")
    sent, grad_out = call(
        gradient_kernel, [slices, full16], [sums, attn, target, gain, weight, turned], narrow, "gradient"
    )
    arrived_back = exchange(sent, "ctx")
    grad_q, local_k, local_v, payoff, gain_out = call(
        local_gradient_kernel,
        [full16, full16, full16, row, shape((HEADS, HEAD_DIM), F32)],
        [grad_out, queries, keys, values, states, cum, columns, sums, arrived_back],
        6 * wide,
        "local_gradient",
        far=(2, 3),
        scratch=pair,
    )
    [later] = call(backward_scan_kernel, [back], [arrived_back, arrived], 1000, "backward_scan")
    later = exchange(later.reshape(BLOCKS, 8, HEAD_DIM), "ctx").reshape(TOK, HEAD_DIM)
    grad_k, grad_v = call(
        final_kernel,
        [full16, full16],
        [later, keys, values, local_k, local_v, columns],
        2 * narrow,
        "final",
        far_outs=(0, 1),
        scratch=pair[:2] + [pltpu.SemaphoreType.DMA((2 * HEADS,))],
    )
    return payoff.reshape(-1), grad_q, grad_k, grad_v, gain_out.reshape(-1)


def solution(mesh):
    placed = (
        P("ctx", "head"),
        P("ctx", "head"),
        P("ctx", "head"),
        P("head", "ctx"),
        P("ctx", "head"),
        P("head"),
        P("ctx"),
    )
    return jax.shard_map(
        local_part,
        mesh=mesh,
        in_specs=placed,
        out_specs=(P("ctx"), P("ctx", "head"), P("ctx", "head"), P("ctx", "head"), P("head")),
        check_vma=False,
    )
```

time: 103 us -> 102 us (level)
  blocking collectives: 58.9 us -> 75.2 us
  starting transfers between devices: 12.2 us -> 5.55 us
  waiting for transfers between devices: 11.2 us -> 5.32 us
  Pallas kernels: 16.4 us -> 12.4 us
  local copies, waits for them, and re-layouts: 2.52 us -> 1.06 us
    all_to_all x3 -> x4, blocking collectives: 58.9 us -> 75.2 us  [exchange(): return lax.all_to_all(x, axis, 0, 0, tiled=True)]
    all_to_all x2 -> x1, starting transfers between devices: 12.2 us -> 5.55 us  [exchange(): return lax.all_to_all(x, axis, 0, 0, tiled=True)]
    all_to_all x2 -> x1, waiting for transfers between devices: 11.2 us -> 5.32 us  [exchange(): return lax.all_to_all(x, axis, 0, 0, tiled=True)]
    pallas_call x8 -> x7, Pallas kernels: 16.4 us -> 12.4 us  [call(): pl.pallas_call(kernel, out_shape=outs, in_specs=[FAR_AWAY if i in far els...]
    unnamed x20 -> x12, local copies, waits for them, and re-layouts: 2.52 us -> 1.06 us
  transfers between devices with their start and end apart: 2 -> 1, of which waited for: 2 -> 1; matrix products, arithmetic and copies ran while one was open for 0% -> 0% of each run, Pallas kernels for 9% -> 5%
where the time goes in v3:
time: 102 us; the launch traced here: 100 us
  blocking collectives  75.2 us (74%)
  Pallas kernels  12.4 us (12%)
  starting transfers between devices  5.55 us (5%)
  waiting for transfers between devices  5.32 us (5%)
  local copies, waits for them, and re-layouts  1.06 us (1%)
    all_to_all x4, blocking collectives, exchange(): return lax.all_to_all(x, axis, 0, 0, tiled=True)  75.2 us
    pallas_call x7, Pallas kernels, call(): pl.pallas_call(kernel, out_shape=outs, in_specs=[FAR_AWAY if i in far els...  12.4 us
    all_to_all x1, starting transfers between devices, exchange(): return lax.all_to_all(x, axis, 0, 0, tiled=True)  5.55 us
    all_to_all x1, waiting for transfers between devices, exchange(): return lax.all_to_all(x, axis, 0, 0, tiled=True)  5.32 us
  transfers between devices with their start and end apart: 1, of which 1 were waited for; matrix products, arithmetic and copies ran while one was open for 0% of the time, Pallas kernels for 5%

profile of v3, /device:TPU:1, one launch (start us, length us, event | category | flops | bytes accessed | tf_op | source)
XLA Modules:
  0.0 100.2 jit_solution(16503471133863009049)
XLA Ops:
  0.6 0.0 copy-start.3
  0.6 1.7 %summary.1 = (bf16[64,16,128]{2,1,0:T(8,128)(2,1)S(1)}, f32[8,512]{1,0:T(8,128)S(1)}, bf16[512,512]{1,0:T(8,128)(2,1)S(1)}, bf16[512,512]{1,0:T(8,128)(2,1)S(1)}...) custom-call(f32[4,512]{1,0:T(4,128)} %retention_far.1, bf16[512,512]{1,0:T(8,128)(2,1)} %keys.1, bf16[512,512]{1,0:T(8,128)(2,1)} %values.1, ...), custom_call_target="tpu_custom_call" | custom-call | flops 67108864 | bytes 2392064 | tf_op jit(solution)/shard_map/summary/pallas_call | solution.py:271
  2.3 0.0 copy-start
  2.3 29.6 %all_to_all.25.arrived.decays = bf16[64,16,128]{2,1,0:T(8,128)(2,1)S(1)} all-to-all(bf16[64,16,128]{2,1,0:T(8,128)(2,1)S(1)} %get-tuple-element.27), channel_id=1, replica_groups=mesh['ctx'=64,'head'=8] {'ctx'}, dimensions={0} | all-to-all | bytes 524288 | tf_op jit(solution)/shard_map/all_to_all | solution.py:288
  32.0 0.0 copy-done.3
  32.0 0.0 copy-done
  32.0 1.7 %local.1 = (bf16[512,128]{1,0:T(8,128)(2,1)S(1)}, f32[512,512]{1,0:T(8,128)S(1)}, bf16[512,512]{1,0:T(8,128)(2,1)S(1)}, f32[512,128]{1,0:T(8,128)S(1)}, f32[1,512]{1,0:T(1,128)S(1)}) custom-call(bf16[64,16,128]{2,1,0:T(8,128)(2,1)S(1)} %all_to_all.25.arrived.decays, bf16[512,512]{1,0:T(8,128)(2,1)S(1)} %copy-done.3, ...), custom_call_target="tpu_custom_call" | custom-call | flops 536870912 | bytes 4343808 | tf_op jit(solution)/shard_map/local/pallas_call | solution.py:271
  33.7 17.2 %all_to_all.26 = bf16[64,8,128]{2,1,0:T(8,128)(2,1)S(1)} all-to-all(bf16[64,8,128]{2,1,0:T(8,128)(2,1)S(1)} %bitcast.11), channel_id=1, replica_groups=mesh['ctx'=64,'head'=8] {'ctx'}, dimensions={0} | all-to-all | bytes 262144 | tf_op jit(solution)/shard_map/all_to_all | solution.py:288
  50.8 0.8 output.1
  51.7 11.6 %all_to_all.27.sums = f32[8,4,512]{2,1,0:T(4,128)S(1)} all-to-all(f32[8,4,512]{2,1,0:T(4,128)S(1)} %get-tuple-element.36), channel_id=1, replica_groups=mesh['ctx'=64,'head'=8] {'head'}, dimensions={0} | all-to-all | bytes 131072 | tf_op jit(solution)/shard_map/all_to_all | solution.py:288
  63.3 1.0 gradient.1
  64.3 0.0 copy-start.4
  64.3 16.8 %all_to_all.28.arrived = bf16[64,16,128]{2,1,0:T(8,128)(2,1)S(1)} all-to-all(bf16[64,16,128]{2,1,0:T(8,128)(2,1)S(1)} %get-tuple-element.41), channel_id=1, replica_groups=mesh['ctx'=64,'head'=8] {'ctx'}, dimensions={0} | all-to-all | bytes 524288 | tf_op jit(solution)/shard_map/all_to_all | solution.py:288
  81.1 0.8 backward_scan.1
  81.9 0.0 copy-done.4
  81.9 5.5 %all-to-all-start.4 = ((bf16[64,8,128]{2,1,0:T(8,128)(2,1)}), bf16[64,8,128]{2,1,0:T(8,128)(2,1)S(1)}, u32[]{:S(2)}, u32[]{:S(2)}) async-start(bf16[64,8,128]{2,1,0:T(8,128)(2,1)} %bitcast.5), calls=%async_computation.4 | async-start | bytes 262144 | tf_op jit(solution)/shard_map/all_to_all | solution.py:288
  87.4 0.0 copy-start.5
  87.5 1.0 %copy-done.5 = bf16[512,512]{1,0:T(8,128)(2,1)S(1)} copy-done((bf16[512,512]{1,0:T(8,128)(2,1)S(1)}, bf16[512,512]{1,0:T(8,128)(2,1)}, u32[]{:S(2)}) %copy-start.5) | copy-done | bytes 524312
  88.5 0.0 copy-start.1
  88.5 0.0 copy-start.2
  88.5 5.1 %local_gradient.1 = (bf16[512,512]{1,0:T(8,128)(2,1)}, bf16[512,512]{1,0:T(8,128)(2,1)S(1)}, bf16[512,512]{1,0:T(8,128)(2,1)S(1)}, f32[1,512]{1,0:T(1,128)}, f32[4,128]{1,0:T(4,128)}) custom-call(bf16[512,512]{1,0:T(8,128)(2,1)S(1)} %copy-done.5, bf16[512,512]{1,0:T(8,128)(2,1)S(1)} %copy-done.3, bf16[512,512]{1,0:T(8,128)(2,1)} %keys.1, ...), custom_call_target="tpu_custom_call" | custom-call | flops 1610612736 | bytes 4411392 | tf_op jit(solution)/shard_map/local_gradient/pallas_call | solution.py:271
  93.6 5.3 %all-to-all-done.4 = bf16[64,8,128]{2,1,0:T(8,128)(2,1)S(1)} async-done(((bf16[64,8,128]{2,1,0:T(8,128)(2,1)}), bf16[64,8,128]{2,1,0:T(8,128)(2,1)S(1)}, u32[]{:S(2)}, u32[]{:S(2)}) %all-to-all-start.4) | async-done | bytes 131104 | tf_op jit(solution)/shard_map/all_to_all | solution.py:288
  99.0 0.0 copy-done.1
  99.0 0.0 copy-done.2
  99.0 1.3 %final.1 = (bf16[512,512]{1,0:T(8,128)(2,1)}, bf16[512,512]{1,0:T(8,128)(2,1)}) custom-call(bf16[512,128]{1,0:T(8,128)(2,1)S(1)} %bitcast.10, bf16[512,512]{1,0:T(8,128)(2,1)S(1)} %copy-done.1, bf16[512,512]{1,0:T(8,128)(2,1)S(1)} %copy-done.2, bf16[512,512]{1,0:T(8,128)(2,1)S(1)} %get-tuple-element.44.local_k, ...), custom_call_target="tpu_custom_call" | custom-call | flops 134217728 | bytes 3538944 | tf_op jit(solution)/shard_map/final/pallas_call | solution.py:271
Async XLA Ops:
  0.6 31.3 %copy-start.3 = (bf16[512,512]{1,0:T(8,128)(2,1)S(1)}, bf16[512,512]{1,0:T(8,128)(2,1)}, u32[]{:S(2)}) copy-start(bf16[512,512]{1,0:T(8,128)(2,1)} %queries.5) | copy-start | bytes 1572868
  2.3 29.7 %copy-start = (bf16[512,512]{1,0:T(8,128)(2,1)S(1)}, bf16[512,512]{1,0:T(8,128)(2,1)}, u32[]{:S(2)}) copy-start(bf16[512,512]{1,0:T(8,128)(2,1)} %target.5) | copy-start | bytes 1572868
  64.3 17.6 %copy-start.4 = (bf16[512,512]{1,0:T(8,128)(2,1)}, bf16[512,512]{1,0:T(8,128)(2,1)S(1)}, u32[]{:S(2)}) copy-start(bf16[512,512]{1,0:T(8,128)(2,1)S(1)} %get-tuple-element.40.grad_out) | copy-start | bytes 1572868
  81.9 17.1 %all-to-all-start.4 = ((bf16[64,8,128]{2,1,0:T(8,128)(2,1)}), bf16[64,8,128]{2,1,0:T(8,128)(2,1)S(1)}, u32[]{:S(2)}, u32[]{:S(2)}) async-start(bf16[64,8,128]{2,1,0:T(8,128)(2,1)} %bitcast.5), calls=%async_computation.4 | async-start | bytes 262144 | tf_op jit(solution)/shard_map/all_to_all | solution.py:288
  87.4 1.0 %copy-start.5 = (bf16[512,512]{1,0:T(8,128)(2,1)S(1)}, bf16[512,512]{1,0:T(8,128)(2,1)}, u32[]{:S(2)}) copy-start(bf16[512,512]{1,0:T(8,128)(2,1)} %copy-done.4) | copy-start | bytes 1572868
  88.5 10.5 %copy-start.1 = (bf16[512,512]{1,0:T(8,128)(2,1)S(1)}, bf16[512,512]{1,0:T(8,128)(2,1)}, u32[]{:S(2)}) copy-start(bf16[512,512]{1,0:T(8,128)(2,1)} %keys.1) | copy-start | bytes 1572868
  88.5 10.5 %copy-start.2 = (bf16[512,512]{1,0:T(8,128)(2,1)S(1)}, bf16[512,512]{1,0:T(8,128)(2,1)}, u32[]{:S(2)}) copy-start(bf16[512,512]{1,0:T(8,128)(2,1)} %values.1) | copy-start | bytes 1572868

commit v4 on v3

--- a/solution.py
+++ b/solution.py
@@ -51,14 +51,19 @@
 
 def aux_tile(row):
     hi, mid, lo = pieces(row)
-    at = lax.broadcasted_iota(jnp.int32, (8, HEAD_DIM), 0)
+    at = lax.broadcasted_iota(jnp.int32, (4, HEAD_DIM), 0)
     return jnp.where(at == 0, hi, jnp.where(at == 1, mid, jnp.where(at == 2, lo, 0.0)))
 
 
 def message(matrix, tile):
     data = matrix.reshape(PER_HEAD, 8, HEAD_DIM)
-    aux = jnp.broadcast_to(tile[None], (PER_HEAD, 8, HEAD_DIM))
-    return jnp.concatenate([data, aux], axis=1).astype(BF16)
+    aux = jnp.broadcast_to(tile[None], (PER_HEAD, 4, HEAD_DIM))
+    return jnp.concatenate([data[:, 0:4], data[:, 4:8], aux], axis=2).astype(BF16)
+
+
+def received(slices, b):
+    got = slices[b].astype(F32)
+    return jnp.concatenate([got[:, 0:128], got[:, 128:256]], axis=0), got[:, 256:384]
 
 
 def summary_kernel(
@@ -92,12 +97,14 @@
     tail = jnp.exp(offset - cum)
     decay = jnp.broadcast_to(jnp.exp(offset), (8, HEAD_DIM))
     got_keys.wait()
+    decayed = []
+    for h in range(HEADS):
+        turned = keys[:, head(h)].T
+        decayed.append((turned.astype(F32) * tail[h : h + 1]).astype(BF16))
     got_values.wait()
     for h in range(HEADS):
-        turned = keys[:, head(h)].T
-        key_decayed = (turned.astype(F32) * tail[h : h + 1]).astype(BF16)
         out[h * PER_HEAD : (h + 1) * PER_HEAD] = message(
-            mm(key_decayed, values[:, head(h)]), aux_tile(decay[h : h + 1])
+            mm(decayed[h], values[:, head(h)]), aux_tile(decay[h : h + 1])
         )
     got_gain.wait()
     got_weight.wait()
@@ -113,8 +120,8 @@
         both = []
         for b in (2 * pair, 2 * pair + 1):
             both.append(state)
-            got = arrived[b].astype(F32)
-            state = decay_rows(got[8:16]) * state + got[0:8]
+            data, aux = received(arrived, b)
+            state = decay_rows(aux) * state + data
         out[16 * pair : 16 * pair + 16] = jnp.concatenate(both, axis=0).astype(BF16)
 
 
@@ -124,7 +131,7 @@
         both = []
         for b in (2 * pair + 1, 2 * pair):
             both.append(state)
-            state = decay_rows(decays[b].astype(F32)[8:16]) * state + arrived[b].astype(F32)[0:8]
+            state = decay_rows(received(decays, b)[1]) * state + received(arrived, b)[0]
         out[16 * pair : 16 * pair + 16] = jnp.concatenate(both[::-1], axis=0).astype(BF16)
 
 
@@ -181,6 +188,17 @@
         sums[d] = four
 
 
+def spread(*rows):
+    parts = [p for row in rows for p in pieces(row)]
+    parts.append(jnp.zeros((16 - len(parts), TOK), F32))
+    width = len(rows) * HEAD_DIM
+    part = lax.broadcasted_iota(jnp.int32, (16, width), 0)
+    first = lax.broadcasted_iota(jnp.int32, (16, width), 1) // HEAD_DIM * 3
+    chosen = jnp.where((part >= first) & (part < first + 3), 1.0, 0.0).astype(BF16)
+    wide = mm(jnp.concatenate(parts, axis=0).astype(BF16), chosen, TN)
+    return [wide[:, head(i)] for i in range(len(rows))]
+
+
 def gradient_kernel(sums, attn, target, gain, weight, turned, out, grad_out):
     four = jnp.sum(sums[...], axis=0)
     mean_square = four[0:1] / HIDDEN_DIMENSION + EPS
@@ -191,8 +209,7 @@
     a = weight[...] / mean_square
     b = weight[...] * inverse
     c = inner / (HIDDEN_DIMENSION * mean_square)
-    side = jnp.concatenate([a, b, c, jnp.zeros((125, TOK), F32)], axis=0).T
-    a, b, c = side[:, 0:1], side[:, 1:2], side[:, 2:3]
+    a, b, c = spread(a, b, c)
     gains, backs = [], []
     for h in range(HEADS):
         o, x, g = attn[:, head(h)], target[:, head(h)].astype(F32), gain[:, head(h)]
@@ -201,9 +218,7 @@
         d = (error * g - c * o).astype(BF16)
         grad_out[:, head(h)] = d
         backs.append(mm(turned[head(h), :], d))
-    gains = jnp.concatenate(gains, axis=0)
-    high = gains.astype(BF16).astype(F32)
-    tile = jnp.concatenate([high, gains - high], axis=0)
+    tile = jnp.concatenate(gains, axis=0)
     for h in range(HEADS):
         out[h * PER_HEAD : (h + 1) * PER_HEAD] = message(backs[h], tile)
 
@@ -220,10 +235,10 @@
     pred_square = four[1:2] / mean_square
     pred_cross = four[2:3] / jnp.sqrt(mean_square)
     payoff[...] = (pred_square - 2.0 * pred_cross + four[3:4]) / HIDDEN_DIMENSION
-    gains = jnp.zeros((8, HEAD_DIM), F32)
+    gains = jnp.zeros((HEADS, HEAD_DIM), F32)
     for b in range(BLOCKS):
-        gains = gains + arrived[b].astype(F32)[8:16]
-    gain_out[...] = (gains[0:HEADS] + gains[HEADS : 2 * HEADS]) / (BLOCKS * TOK)
+        gains = gains + received(arrived, b)[1]
+    gain_out[...] = gains / (BLOCKS * TOK)
     got_keys.wait()
     got_values.wait()
     for h in range(HEADS):
@@ -293,7 +308,7 @@
     narrow = TOK * HEAD_DIM * HEAD_DIM * 2 * HEADS
     gain = gain.reshape(1, -1)
     weight = weight.reshape(1, -1)
-    slices = shape((BLOCKS, 16, HEAD_DIM), BF16)
+    slices = shape((BLOCKS, 4, 3 * HEAD_DIM), BF16)
     full32 = shape((TOK, TOK), F32)
     full16 = shape((TOK, TOK), BF16)
     row = shape((1, TOK), F32)

time: 102 us -> 99 us (0.971)
  blocking collectives: 75.2 us -> 72.8 us
    all_to_all x4, blocking collectives: 75.2 us -> 72.8 us  [exchange(): return lax.all_to_all(x, axis, 0, 0, tiled=True)]
where the time goes in v4:
time: 99 us; the launch traced here: 97.5 us
  blocking collectives  72.8 us (74%)
  Pallas kernels  12.4 us (13%)
  waiting for transfers between devices  5.3 us (5%)
  starting transfers between devices  5.22 us (5%)
  local copies, waits for them, and re-layouts  1.06 us (1%)
    all_to_all x4, blocking collectives, exchange(): return lax.all_to_all(x, axis, 0, 0, tiled=True)  72.8 us
    pallas_call x7, Pallas kernels, call(): pl.pallas_call(kernel, out_shape=outs, in_specs=[FAR_AWAY if i in far els...  12.4 us
    all_to_all x1, waiting for transfers between devices, exchange(): return lax.all_to_all(x, axis, 0, 0, tiled=True)  5.3 us
    all_to_all x1, starting transfers between devices, exchange(): return lax.all_to_all(x, axis, 0, 0, tiled=True)  5.22 us
  transfers between devices with their start and end apart: 1, of which 1 were waited for; matrix products, arithmetic and copies ran while one was open for 0% of the time, Pallas kernels for 5%

profile of v4, /device:TPU:1, one launch (start us, length us, event | category | flops | bytes accessed | tf_op | source)
XLA Modules:
  0.0 97.5 jit_solution(10514671146487532158)
XLA Ops:
  0.6 0.0 copy-start
  0.6 0.0 copy-start.3
  0.7 1.8 %summary.1 = (bf16[64,4,384]{2,1,0:T(4,128)(2,1)S(1)}, f32[8,512]{1,0:T(8,128)S(1)}, bf16[512,512]{1,0:T(8,128)(2,1)S(1)}, bf16[512,512]{1,0:T(8,128)(2,1)S(1)},...) custom-call(f32[4,512]{1,0:T(4,128)} %retention_far.1, bf16[512,512]{1,0:T(8,128)(2,1)} %keys.1, bf16[512,512]{1,0:T(8,128)(2,1)} %values.1, ...), custom_call_target="tpu_custom_call" | custom-call | flops 67108864 | bytes 2326528 | tf_op jit(solution)/shard_map/summary/pallas_call | solution.py:286
  2.4 28.8 %all_to_all.25.arrived.decays = bf16[64,4,384]{2,1,0:T(4,128)(2,1)S(1)} all-to-all(bf16[64,4,384]{2,1,0:T(4,128)(2,1)S(1)} %get-tuple-element.27), channel_id=1, replica_groups=mesh['ctx'=64,'head'=8] {'ctx'}, dimensions={0} | all-to-all | bytes 393216 | tf_op jit(solution)/shard_map/all_to_all | solution.py:303
  31.2 0.0 copy-done
  31.2 0.0 copy-done.3
  31.2 1.7 %local.1 = (bf16[512,128]{1,0:T(8,128)(2,1)S(1)}, f32[512,512]{1,0:T(8,128)S(1)}, bf16[512,512]{1,0:T(8,128)(2,1)S(1)}, f32[512,128]{1,0:T(8,128)S(1)}, f32[1,512]{1,0:T(1,128)S(1)}) custom-call(bf16[64,4,384]{2,1,0:T(4,128)(2,1)S(1)} %all_to_all.25.arrived.decays, bf16[512,512]{1,0:T(8,128)(2,1)S(1)} %copy-done.3, ...), custom_call_target="tpu_custom_call" | custom-call | flops 536870912 | bytes 4278272 | tf_op jit(solution)/shard_map/local/pallas_call | solution.py:286
  32.9 16.6 %all_to_all.26 = bf16[64,8,128]{2,1,0:T(8,128)(2,1)S(1)} all-to-all(bf16[64,8,128]{2,1,0:T(8,128)(2,1)S(1)} %bitcast.11), channel_id=1, replica_groups=mesh['ctx'=64,'head'=8] {'ctx'}, dimensions={0} | all-to-all | bytes 262144 | tf_op jit(solution)/shard_map/all_to_all | solution.py:303
  49.5 0.8 output.1
  50.3 11.8 %all_to_all.27.sums = f32[8,4,512]{2,1,0:T(4,128)S(1)} all-to-all(f32[8,4,512]{2,1,0:T(4,128)S(1)} %get-tuple-element.36), channel_id=1, replica_groups=mesh['ctx'=64,'head'=8] {'head'}, dimensions={0} | all-to-all | bytes 131072 | tf_op jit(solution)/shard_map/all_to_all | solution.py:303
  62.1 0.9 gradient.1
  63.0 0.0 copy-start.4
  63.0 15.7 %all_to_all.28.arrived = bf16[64,4,384]{2,1,0:T(4,128)(2,1)S(1)} all-to-all(bf16[64,4,384]{2,1,0:T(4,128)(2,1)S(1)} %get-tuple-element.41), channel_id=1, replica_groups=mesh['ctx'=64,'head'=8] {'ctx'}, dimensions={0} | all-to-all | bytes 393216 | tf_op jit(solution)/shard_map/all_to_all | solution.py:303
  78.7 0.8 backward_scan.1
  79.5 0.0 copy-done.4
  79.5 5.2 %all-to-all-start.4 = ((bf16[64,8,128]{2,1,0:T(8,128)(2,1)}), bf16[64,8,128]{2,1,0:T(8,128)(2,1)S(1)}, u32[]{:S(2)}, u32[]{:S(2)}) async-start(bf16[64,8,128]{2,1,0:T(8,128)(2,1)} %bitcast.5), calls=%async_computation.4 | async-start | bytes 262144 | tf_op jit(solution)/shard_map/all_to_all | solution.py:303
  84.7 0.0 copy-start.5
  84.7 1.0 %copy-done.5 = bf16[512,512]{1,0:T(8,128)(2,1)S(1)} copy-done((bf16[512,512]{1,0:T(8,128)(2,1)S(1)}, bf16[512,512]{1,0:T(8,128)(2,1)}, u32[]{:S(2)}) %copy-start.5) | copy-done | bytes 524312
  85.7 0.0 copy-start.1
  85.7 0.0 copy-start.2
  85.7 5.1 %local_gradient.1 = (bf16[512,512]{1,0:T(8,128)(2,1)}, bf16[512,512]{1,0:T(8,128)(2,1)S(1)}, bf16[512,512]{1,0:T(8,128)(2,1)S(1)}, f32[1,512]{1,0:T(1,128)}, f32[4,128]{1,0:T(4,128)}) custom-call(bf16[512,512]{1,0:T(8,128)(2,1)S(1)} %copy-done.5, bf16[512,512]{1,0:T(8,128)(2,1)S(1)} %copy-done.3, bf16[512,512]{1,0:T(8,128)(2,1)} %keys.1, ...), custom_call_target="tpu_custom_call" | custom-call | flops 1610612736 | bytes 4345856 | tf_op jit(solution)/shard_map/local_gradient/pallas_call | solution.py:286
  90.9 5.3 %all-to-all-done.4 = bf16[64,8,128]{2,1,0:T(8,128)(2,1)S(1)} async-done(((bf16[64,8,128]{2,1,0:T(8,128)(2,1)}), bf16[64,8,128]{2,1,0:T(8,128)(2,1)S(1)}, u32[]{:S(2)}, u32[]{:S(2)}) %all-to-all-start.4) | async-done | bytes 131104 | tf_op jit(solution)/shard_map/all_to_all | solution.py:303
  96.2 0.0 copy-done.1
  96.2 0.0 copy-done.2
  96.2 1.3 %final.1 = (bf16[512,512]{1,0:T(8,128)(2,1)}, bf16[512,512]{1,0:T(8,128)(2,1)}) custom-call(bf16[512,128]{1,0:T(8,128)(2,1)S(1)} %bitcast.10, bf16[512,512]{1,0:T(8,128)(2,1)S(1)} %copy-done.1, bf16[512,512]{1,0:T(8,128)(2,1)S(1)} %copy-done.2, bf16[512,512]{1,0:T(8,128)(2,1)S(1)} %get-tuple-element.44.local_k, ...), custom_call_target="tpu_custom_call" | custom-call | flops 134217728 | bytes 3538944 | tf_op jit(solution)/shard_map/final/pallas_call | solution.py:286
Async XLA Ops:
  0.6 30.6 %copy-start = (bf16[512,512]{1,0:T(8,128)(2,1)S(1)}, bf16[512,512]{1,0:T(8,128)(2,1)}, u32[]{:S(2)}) copy-start(bf16[512,512]{1,0:T(8,128)(2,1)} %target.5) | copy-start | bytes 1572868
  0.6 30.6 %copy-start.3 = (bf16[512,512]{1,0:T(8,128)(2,1)S(1)}, bf16[512,512]{1,0:T(8,128)(2,1)}, u32[]{:S(2)}) copy-start(bf16[512,512]{1,0:T(8,128)(2,1)} %queries.5) | copy-start | bytes 1572868
  63.0 16.5 %copy-start.4 = (bf16[512,512]{1,0:T(8,128)(2,1)}, bf16[512,512]{1,0:T(8,128)(2,1)S(1)}, u32[]{:S(2)}) copy-start(bf16[512,512]{1,0:T(8,128)(2,1)S(1)} %get-tuple-element.40.grad_out) | copy-start | bytes 1572868
  79.5 16.7 %all-to-all-start.4 = ((bf16[64,8,128]{2,1,0:T(8,128)(2,1)}), bf16[64,8,128]{2,1,0:T(8,128)(2,1)S(1)}, u32[]{:S(2)}, u32[]{:S(2)}) async-start(bf16[64,8,128]{2,1,0:T(8,128)(2,1)} %bitcast.5), calls=%async_computation.4 | async-start | bytes 262144 | tf_op jit(solution)/shard_map/all_to_all | solution.py:303
  84.7 1.0 %copy-start.5 = (bf16[512,512]{1,0:T(8,128)(2,1)S(1)}, bf16[512,512]{1,0:T(8,128)(2,1)}, u32[]{:S(2)}) copy-start(bf16[512,512]{1,0:T(8,128)(2,1)} %copy-done.4) | copy-start | bytes 1572868
  85.7 10.5 %copy-start.1 = (bf16[512,512]{1,0:T(8,128)(2,1)S(1)}, bf16[512,512]{1,0:T(8,128)(2,1)}, u32[]{:S(2)}) copy-start(bf16[512,512]{1,0:T(8,128)(2,1)} %keys.1) | copy-start | bytes 1572868
  85.7 10.5 %copy-start.2 = (bf16[512,512]{1,0:T(8,128)(2,1)S(1)}, bf16[512,512]{1,0:T(8,128)(2,1)}, u32[]{:S(2)}) copy-start(bf16[512,512]{1,0:T(8,128)(2,1)} %values.1) | copy-start | bytes 1572868

commit v5 on v4

--- a/solution.py
+++ b/solution.py
@@ -16,6 +16,8 @@
 BLOCKS = 64
 PER_HEAD = BLOCKS // HEADS
 HALF = TOK // 2
+HALVES = EARLY, LATE = slice(0, HALF), slice(HALF, TOK)
+TILES = (0, 0), (1, 0), (1, 1)
 FAR = -1e9
 LOG2E = math.log2(math.e)
 LOG2_SCALE = math.log2(SCALE)
@@ -135,13 +137,26 @@
         out[16 * pair : 16 * pair + 16] = jnp.concatenate(both[::-1], axis=0).astype(BF16)
 
 
-def block_decay(logs, columns, h, i):
-    rows, width = slice(i * HALF, (i + 1) * HALF), (i + 1) * HALF
-    gap = columns[rows, h : h + 1] - logs[h : h + 1, 0:width]
-    t = lax.broadcasted_iota(jnp.int32, (HALF, HALF), 0)
-    s = lax.broadcasted_iota(jnp.int32, (HALF, HALF), 1)
-    last = jnp.where(s <= t, gap[:, i * HALF :], FAR)
-    return jnp.exp2(last if i == 0 else jnp.concatenate([gap[:, 0:HALF], last], axis=1))
+def block_decay(logs, columns, h, i, j):
+    gap = columns[HALVES[i], h : h + 1] - logs[h : h + 1, HALVES[j]]
+    if i == j:
+        t = lax.broadcasted_iota(jnp.int32, (HALF, HALF), 0)
+        s = lax.broadcasted_iota(jnp.int32, (HALF, HALF), 1)
+        gap = jnp.where(s <= t, gap, FAR)
+    return jnp.exp2(gap)
+
+
+def products(a, b):
+    first = mm(a, b[EARLY], NT)
+    return first[EARLY], first[LATE], mm(a[LATE], b[LATE], NT)
+
+
+def along_rows(tiles, b):
+    return mm(tiles[0], b[EARLY]), mm(jnp.concatenate(tiles[1:], axis=1), b)
+
+
+def along_columns(tiles, b):
+    return mm(jnp.concatenate(tiles[:2], axis=0), b, TN), mm(tiles[2], b[LATE], TN)
 
 
 def local_kernel(
@@ -154,16 +169,20 @@
     logs = cum[...] * LOG2E
     side = jnp.concatenate([logs + LOG2_SCALE, start, tail, jnp.zeros((104, TOK), F32)], axis=0).T
     columns[...] = side
+    probs = []
+    for h in range(HEADS):
+        scores = products(queries[:, head(h)], keys[:, head(h)])
+        probs.append(
+            [(a * block_decay(logs, side, h, *tile)).astype(BF16) for a, tile in zip(scores, TILES)]
+        )
+    for h in range(HEADS):
+        for rows, part in zip(HALVES, along_rows(probs[h], values[:, head(h)])):
+            local[rows, head(h)] = part
     square = jnp.zeros((TOK, HEAD_DIM), F32)
     for h in range(HEADS):
         x = target[:, head(h)].astype(F32)
         square = square + x * x
-        q, k, v = queries[:, head(h)], keys[:, head(h)], values[:, head(h)]
-        turned[head(h), :] = (q.T.astype(F32) * start[h : h + 1]).astype(BF16)
-        for i in range(2):
-            rows, width = slice(i * HALF, (i + 1) * HALF), (i + 1) * HALF
-            p = (mm(q[rows], k[0:width], NT) * block_decay(logs, side, h, i)).astype(BF16)
-            local[rows, head(h)] = mm(p, v[0:width])
+        turned[head(h), :] = (queries[:, head(h)].T.astype(F32) * start[h : h + 1]).astype(BF16)
     target_square[...] = jnp.sum(square.T, axis=0, keepdims=True)
 
 
@@ -171,9 +190,9 @@
     square = jnp.zeros((TOK, HEAD_DIM), F32)
     gain_square = square
     cross = square
-    for h in range(HEADS):
-        carried = mm(queries[:, head(h)], states[head(h), :])
-        o = local[:, head(h)] + columns[:, 8 + h : 9 + h] * carried
+    carried = [mm(queries[:, head(h)], states[head(h), :]) for h in range(HEADS)]
+    for h in range(HEADS):
+        o = local[:, head(h)] + columns[:, 8 + h : 9 + h] * carried[h]
         attn[:, head(h)] = o
         gained = gain[:, head(h)] * o
         square = square + o * o
@@ -244,18 +263,14 @@
     for h in range(HEADS):
         q, k, v, d = queries[:, head(h)], keys[:, head(h)], values[:, head(h)], grad_out[:, head(h)]
         carried = columns[:, 8 + h : 9 + h] * mm(d, states[head(h), :], NT)
-        parts, probs = [], []
-        for i in range(2):
-            rows, width = slice(i * HALF, (i + 1) * HALF), (i + 1) * HALF
-            decay = block_decay(logs, columns, h, i)
-            probs.append((mm(q[rows], k[0:width], NT) * decay).astype(BF16))
-            gp = (mm(d[rows], v[0:width], NT) * decay).astype(BF16)
-            parts.append(gp)
-            grad_q[rows, head(h)] = (mm(gp, k[0:width]) + carried[rows]).astype(BF16)
-        for side, near, far in ((local_k, parts, q), (local_v, probs, d)):
-            early = jnp.concatenate([near[0], near[1][:, 0:HALF]], axis=0)
-            side[0:HALF, head(h)] = mm(early, far, TN).astype(BF16)
-            side[HALF:TOK, head(h)] = mm(near[1][:, HALF:TOK], far[HALF:TOK], TN).astype(BF16)
+        decays = [block_decay(logs, columns, h, *tile) for tile in TILES]
+        probs = [(a * decay).astype(BF16) for a, decay in zip(products(q, k), decays)]
+        grads = [(a * decay).astype(BF16) for a, decay in zip(products(d, v), decays)]
+        for rows, part in zip(HALVES, along_rows(grads, k)):
+            grad_q[rows, head(h)] = (part + carried[rows]).astype(BF16)
+        for side, tiles, far in ((local_k, grads, q), (local_v, probs, d)):
+            for rows, part in zip(HALVES, along_columns(tiles, far)):
+                side[rows, head(h)] = part.astype(BF16)
 
 
 def final_kernel(

time: 99 us -> 98.5 us (level)
  no operation moved by 1% of the time
where the time goes in v5:
time: 98.5 us; the launch traced here: 97 us
  blocking collectives  72.8 us (74%)
  Pallas kernels  11.5 us (12%)
  waiting for transfers between devices  5.69 us (6%)
  starting transfers between devices  5.22 us (5%)
  local copies, waits for them, and re-layouts  1.06 us (1%)
    all_to_all x4, blocking collectives, exchange(): return lax.all_to_all(x, axis, 0, 0, tiled=True)  72.8 us
    pallas_call x7, Pallas kernels, call(): pl.pallas_call(kernel, out_shape=outs, in_specs=[FAR_AWAY if i in far els...  11.5 us
    all_to_all x1, waiting for transfers between devices, exchange(): return lax.all_to_all(x, axis, 0, 0, tiled=True)  5.69 us
    all_to_all x1, starting transfers between devices, exchange(): return lax.all_to_all(x, axis, 0, 0, tiled=True)  5.22 us
  transfers between devices with their start and end apart: 1, of which 1 were waited for; matrix products, arithmetic and copies ran while one was open for 0% of the time, Pallas kernels for 5%

profile of v5, /device:TPU:1, one launch (start us, length us, event | category | flops | bytes accessed | tf_op | source)
XLA Modules:
  0.0 97.0 jit_solution(5359111761023123994)
XLA Ops:
  0.6 0.0 copy-start
  0.6 0.0 copy-start.3
  0.7 1.8 %summary.1 = (bf16[64,4,384]{2,1,0:T(4,128)(2,1)S(1)}, f32[8,512]{1,0:T(8,128)S(1)}, bf16[512,512]{1,0:T(8,128)(2,1)S(1)}, bf16[512,512]{1,0:T(8,128)(2,1)S(1)},...) custom-call(f32[4,512]{1,0:T(4,128)} %retention_far.1, bf16[512,512]{1,0:T(8,128)(2,1)} %keys.1, bf16[512,512]{1,0:T(8,128)(2,1)} %values.1, ...), custom_call_target="tpu_custom_call" | custom-call | flops 67108864 | bytes 2326528 | tf_op jit(solution)/shard_map/summary/pallas_call | solution.py:301
  2.4 28.8 %all_to_all.25.arrived.decays = bf16[64,4,384]{2,1,0:T(4,128)(2,1)S(1)} all-to-all(bf16[64,4,384]{2,1,0:T(4,128)(2,1)S(1)} %get-tuple-element.27), channel_id=1, replica_groups=mesh['ctx'=64,'head'=8] {'ctx'}, dimensions={0} | all-to-all | bytes 393216 | tf_op jit(solution)/shard_map/all_to_all | solution.py:318
  31.2 0.0 copy-done
  31.2 0.0 copy-done.3
  31.2 1.2 %local.1 = (bf16[512,128]{1,0:T(8,128)(2,1)S(1)}, f32[512,512]{1,0:T(8,128)S(1)}, bf16[512,512]{1,0:T(8,128)(2,1)S(1)}, f32[512,128]{1,0:T(8,128)S(1)}, f32[1,512]{1,0:T(1,128)S(1)}) custom-call(bf16[64,4,384]{2,1,0:T(4,128)(2,1)S(1)} %all_to_all.25.arrived.decays, bf16[512,512]{1,0:T(8,128)(2,1)S(1)} %copy-done.3, ...), custom_call_target="tpu_custom_call" | custom-call | flops 536870912 | bytes 4278272 | tf_op jit(solution)/shard_map/local/pallas_call | solution.py:301
  32.4 16.6 %all_to_all.26 = bf16[64,8,128]{2,1,0:T(8,128)(2,1)S(1)} all-to-all(bf16[64,8,128]{2,1,0:T(8,128)(2,1)S(1)} %bitcast.11), channel_id=1, replica_groups=mesh['ctx'=64,'head'=8] {'ctx'}, dimensions={0} | all-to-all | bytes 262144 | tf_op jit(solution)/shard_map/all_to_all | solution.py:318
  49.0 0.8 output.1
  49.8 11.8 %all_to_all.27.sums = f32[8,4,512]{2,1,0:T(4,128)S(1)} all-to-all(f32[8,4,512]{2,1,0:T(4,128)S(1)} %get-tuple-element.36), channel_id=1, replica_groups=mesh['ctx'=64,'head'=8] {'head'}, dimensions={0} | all-to-all | bytes 131072 | tf_op jit(solution)/shard_map/all_to_all | solution.py:318
  61.6 0.9 gradient.1
  62.5 0.0 copy-start.4
  62.6 15.7 %all_to_all.28.arrived = bf16[64,4,384]{2,1,0:T(4,128)(2,1)S(1)} all-to-all(bf16[64,4,384]{2,1,0:T(4,128)(2,1)S(1)} %get-tuple-element.41), channel_id=1, replica_groups=mesh['ctx'=64,'head'=8] {'ctx'}, dimensions={0} | all-to-all | bytes 393216 | tf_op jit(solution)/shard_map/all_to_all | solution.py:318
  78.2 0.8 backward_scan.1
  79.0 0.0 copy-done.4
  79.0 5.2 %all-to-all-start.4 = ((bf16[64,8,128]{2,1,0:T(8,128)(2,1)}), bf16[64,8,128]{2,1,0:T(8,128)(2,1)S(1)}, u32[]{:S(2)}, u32[]{:S(2)}) async-start(bf16[64,8,128]{2,1,0:T(8,128)(2,1)} %bitcast.5), calls=%async_computation.4 | async-start | bytes 262144 | tf_op jit(solution)/shard_map/all_to_all | solution.py:318
  84.2 0.0 copy-start.5
  84.3 1.0 %copy-done.5 = bf16[512,512]{1,0:T(8,128)(2,1)S(1)} copy-done((bf16[512,512]{1,0:T(8,128)(2,1)S(1)}, bf16[512,512]{1,0:T(8,128)(2,1)}, u32[]{:S(2)}) %copy-start.5) | copy-done | bytes 524312
  85.3 0.0 copy-start.1
  85.3 0.0 copy-start.2
  85.3 4.8 %local_gradient.1 = (bf16[512,512]{1,0:T(8,128)(2,1)}, bf16[512,512]{1,0:T(8,128)(2,1)S(1)}, bf16[512,512]{1,0:T(8,128)(2,1)S(1)}, f32[1,512]{1,0:T(1,128)}, f32[4,128]{1,0:T(4,128)}) custom-call(bf16[512,512]{1,0:T(8,128)(2,1)S(1)} %copy-done.5, bf16[512,512]{1,0:T(8,128)(2,1)S(1)} %copy-done.3, bf16[512,512]{1,0:T(8,128)(2,1)} %keys.1, ...), custom_call_target="tpu_custom_call" | custom-call | flops 1610612736 | bytes 4345856 | tf_op jit(solution)/shard_map/local_gradient/pallas_call | solution.py:301
  90.1 5.7 %all-to-all-done.4 = bf16[64,8,128]{2,1,0:T(8,128)(2,1)S(1)} async-done(((bf16[64,8,128]{2,1,0:T(8,128)(2,1)}), bf16[64,8,128]{2,1,0:T(8,128)(2,1)S(1)}, u32[]{:S(2)}, u32[]{:S(2)}) %all-to-all-start.4) | async-done | bytes 131104 | tf_op jit(solution)/shard_map/all_to_all | solution.py:318
  95.7 0.0 copy-done.1
  95.7 0.0 copy-done.2
  95.8 1.3 %final.1 = (bf16[512,512]{1,0:T(8,128)(2,1)}, bf16[512,512]{1,0:T(8,128)(2,1)}) custom-call(bf16[512,128]{1,0:T(8,128)(2,1)S(1)} %bitcast.10, bf16[512,512]{1,0:T(8,128)(2,1)S(1)} %copy-done.1, bf16[512,512]{1,0:T(8,128)(2,1)S(1)} %copy-done.2, bf16[512,512]{1,0:T(8,128)(2,1)S(1)} %get-tuple-element.44.local_k, ...), custom_call_target="tpu_custom_call" | custom-call | flops 134217728 | bytes 3538944 | tf_op jit(solution)/shard_map/final/pallas_call | solution.py:301
Async XLA Ops:
  0.6 30.6 %copy-start = (bf16[512,512]{1,0:T(8,128)(2,1)S(1)}, bf16[512,512]{1,0:T(8,128)(2,1)}, u32[]{:S(2)}) copy-start(bf16[512,512]{1,0:T(8,128)(2,1)} %target.5) | copy-start | bytes 1572868
  0.6 30.6 %copy-start.3 = (bf16[512,512]{1,0:T(8,128)(2,1)S(1)}, bf16[512,512]{1,0:T(8,128)(2,1)}, u32[]{:S(2)}) copy-start(bf16[512,512]{1,0:T(8,128)(2,1)} %queries.5) | copy-start | bytes 1572868
  62.5 16.5 %copy-start.4 = (bf16[512,512]{1,0:T(8,128)(2,1)}, bf16[512,512]{1,0:T(8,128)(2,1)S(1)}, u32[]{:S(2)}) copy-start(bf16[512,512]{1,0:T(8,128)(2,1)S(1)} %get-tuple-element.40.grad_out) | copy-start | bytes 1572868
  79.0 16.7 %all-to-all-start.4 = ((bf16[64,8,128]{2,1,0:T(8,128)(2,1)}), bf16[64,8,128]{2,1,0:T(8,128)(2,1)S(1)}, u32[]{:S(2)}, u32[]{:S(2)}) async-start(bf16[64,8,128]{2,1,0:T(8,128)(2,1)} %bitcast.5), calls=%async_computation.4 | async-start | bytes 262144 | tf_op jit(solution)/shard_map/all_to_all | solution.py:318
  84.2 1.0 %copy-start.5 = (bf16[512,512]{1,0:T(8,128)(2,1)S(1)}, bf16[512,512]{1,0:T(8,128)(2,1)}, u32[]{:S(2)}) copy-start(bf16[512,512]{1,0:T(8,128)(2,1)} %copy-done.4) | copy-start | bytes 1572868
  85.3 10.5 %copy-start.1 = (bf16[512,512]{1,0:T(8,128)(2,1)S(1)}, bf16[512,512]{1,0:T(8,128)(2,1)}, u32[]{:S(2)}) copy-start(bf16[512,512]{1,0:T(8,128)(2,1)} %keys.1) | copy-start | bytes 1572868
  85.3 10.5 %copy-start.2 = (bf16[512,512]{1,0:T(8,128)(2,1)S(1)}, bf16[512,512]{1,0:T(8,128)(2,1)}, u32[]{:S(2)}) copy-start(bf16[512,512]{1,0:T(8,128)(2,1)} %values.1) | copy-start | bytes 1572868

commit v6 on v5

--- a/solution.py
+++ b/solution.py
@@ -15,6 +15,7 @@
 HEADS = 4
 BLOCKS = 64
 PER_HEAD = BLOCKS // HEADS
+FIRST = {"ctx": 36, "head": 4}
 HALF = TOK // 2
 HALVES = EARLY, LATE = slice(0, HALF), slice(HALF, TOK)
 TILES = (0, 0), (1, 0), (1, 1)
@@ -63,8 +64,12 @@
     return jnp.concatenate([data[:, 0:4], data[:, 4:8], aux], axis=2).astype(BF16)
 
 
+def slot(b):
+    return (b - FIRST["ctx"]) % BLOCKS
+
+
 def received(slices, b):
-    got = slices[b].astype(F32)
+    got = slices[slot(b)].astype(F32)
     return jnp.concatenate([got[:, 0:128], got[:, 128:256]], axis=0), got[:, 256:384]
 
 
@@ -124,7 +129,8 @@
             both.append(state)
             data, aux = received(arrived, b)
             state = decay_rows(aux) * state + data
-        out[16 * pair : 16 * pair + 16] = jnp.concatenate(both, axis=0).astype(BF16)
+        at = 8 * slot(2 * pair)
+        out[at : at + 16] = jnp.concatenate(both, axis=0).astype(BF16)
 
 
 def backward_scan_kernel(arrived, decays, out):
@@ -134,7 +140,8 @@
         for b in (2 * pair + 1, 2 * pair):
             both.append(state)
             state = decay_rows(received(decays, b)[1]) * state + received(arrived, b)[0]
-        out[16 * pair : 16 * pair + 16] = jnp.concatenate(both[::-1], axis=0).astype(BF16)
+        at = 8 * slot(2 * pair)
+        out[at : at + 16] = jnp.concatenate(both[::-1], axis=0).astype(BF16)
 
 
 def block_decay(logs, columns, h, i, j):
@@ -315,7 +322,9 @@
 
 
 def exchange(x, axis):
-    return lax.all_to_all(x, axis, 0, 0, tiled=True)
+    count, first = x.shape[0], FIRST[axis]
+    order = [(first + i) % count for i in range(count)]
+    return lax.all_to_all(x, axis, 0, 0, tiled=True, axis_index_groups=[order])
 
 
 def local_part(queries, keys, values, retention, target, gain, weight):

time: 98.5 us -> 92.6 us (0.940); the launches traced: 97 us -> 92.2 us
  starting transfers between devices: 5.22 us -> 12.7 us
  blocking collectives: 72.8 us -> 66.1 us
  waiting for transfers between devices: 5.69 us -> 0.01 us
    all_to_all x1, starting transfers between devices: 5.22 us -> 12.7 us  [exchange(): return lax.all_to_all(x, axis, 0, 0, tiled=True, axis_index_groups=[order])]
    all_to_all x4, blocking collectives: 72.8 us -> 66.1 us  [exchange(): return lax.all_to_all(x, axis, 0, 0, tiled=True, axis_index_groups=[order])]
    all_to_all x1, waiting for transfers between devices: 5.69 us -> 0.01 us  [exchange(): return lax.all_to_all(x, axis, 0, 0, tiled=True, axis_index_groups=[order])]
  transfers between devices with their start and end apart: 1 -> 1, of which waited for: 1 -> 0; matrix products, arithmetic and copies ran while one was open for 0% -> 0% of each run, Pallas kernels for 5% -> 5%
where the time goes in v6:
time: 92.6 us; the launch traced here: 92.2 us
  blocking collectives  66.1 us (71%)
  starting transfers between devices  12.7 us (14%)
  Pallas kernels  11.6 us (13%)
  local copies, waits for them, and re-layouts  1.06 us (1%)
    all_to_all x4, blocking collectives, exchange(): return lax.all_to_all(x, axis, 0, 0, tiled=True, axis_index_groups=[order])  66.1 us
    all_to_all x1, starting transfers between devices, exchange(): return lax.all_to_all(x, axis, 0, 0, tiled=True, axis_index_groups=[order])  12.7 us
    pallas_call x7, Pallas kernels, call(): pl.pallas_call(kernel, out_shape=outs, in_specs=[FAR_AWAY if i in far els...  11.6 us
  transfers between devices with their start and end apart: 1, of which 0 were waited for; matrix products, arithmetic and copies ran while one was open for 0% of the time, Pallas kernels for 5%

profile of v6, /device:TPU:1, one launch (start us, length us, event | category | flops | bytes accessed | tf_op | source)
XLA Modules:
  0.0 92.2 jit_solution(6751341414627332639)
XLA Ops:
  0.6 0.0 copy-start
  0.6 0.0 copy-start.3
  0.7 1.8 %summary.1 = (bf16[64,4,384]{2,1,0:T(4,128)(2,1)S(1)}, f32[8,512]{1,0:T(8,128)S(1)}, bf16[512,512]{1,0:T(8,128)(2,1)S(1)}, bf16[512,512]{1,0:T(8,128)(2,1)S(1)},...) custom-call(f32[4,512]{1,0:T(4,128)} %retention_far.1, bf16[512,512]{1,0:T(8,128)(2,1)} %keys.1, bf16[512,512]{1,0:T(8,128)(2,1)} %values.1, ...), custom_call_target="tpu_custom_call" | custom-call | flops 67108864 | bytes 2326528 | tf_op jit(solution)/shard_map/summary/pallas_call | solution.py:308
  2.4 24.0 %all_to_all.25.arrived.decays = bf16[64,4,384]{2,1,0:T(4,128)(2,1)S(1)} all-to-all(bf16[64,4,384]{2,1,0:T(4,128)(2,1)S(1)} %get-tuple-element.27), channel_id=1, replica_groups={{288,296,304,312,320,328,336,344,352,360,368,376,384,392,400,408,416,42..., dimensions={0} | all-to-all | bytes 393216 | tf_op jit(solution)/shard_map/all_to_all | solution.py:327
  26.4 0.0 copy-done
  26.4 0.0 copy-done.3
  26.4 1.2 %local.1 = (bf16[512,128]{1,0:T(8,128)(2,1)S(1)}, f32[512,512]{1,0:T(8,128)S(1)}, bf16[512,512]{1,0:T(8,128)(2,1)S(1)}, f32[512,128]{1,0:T(8,128)S(1)}, f32[1,512]{1,0:T(1,128)S(1)}) custom-call(bf16[64,4,384]{2,1,0:T(4,128)(2,1)S(1)} %all_to_all.25.arrived.decays, bf16[512,512]{1,0:T(8,128)(2,1)S(1)} %copy-done.3, ...), custom_call_target="tpu_custom_call" | custom-call | flops 536870912 | bytes 4278272 | tf_op jit(solution)/shard_map/local/pallas_call | solution.py:308
  27.6 15.9 %all_to_all.26 = bf16[64,8,128]{2,1,0:T(8,128)(2,1)S(1)} all-to-all(bf16[64,8,128]{2,1,0:T(8,128)(2,1)S(1)} %bitcast.11), channel_id=1, replica_groups={{288,296,304,312,320,328,336,344,352,360,368,376,384,392,400,408,416,42..., dimensions={0} | all-to-all | bytes 262144 | tf_op jit(solution)/shard_map/all_to_all | solution.py:327
  43.5 0.8 output.1
  44.4 9.3 %all_to_all.27.sums = f32[8,4,512]{2,1,0:T(4,128)S(1)} all-to-all(f32[8,4,512]{2,1,0:T(4,128)S(1)} %get-tuple-element.36), channel_id=1, replica_groups={{4,5,6,7,0,1,2,3},{12,13,14,15,8,9,10,11},{20,21,22,23,16,17,18,19},{28..., dimensions={0} | all-to-all | bytes 131072 | tf_op jit(solution)/shard_map/all_to_all | solution.py:327
  53.7 0.9 gradient.1
  54.6 0.0 copy-start.4
  54.6 16.9 %all_to_all.28.arrived = bf16[64,4,384]{2,1,0:T(4,128)(2,1)S(1)} all-to-all(bf16[64,4,384]{2,1,0:T(4,128)(2,1)S(1)} %get-tuple-element.41), channel_id=1, replica_groups={{288,296,304,312,320,328,336,344,352,360,368,376,384,392,400,408,416,42..., dimensions={0} | all-to-all | bytes 393216 | tf_op jit(solution)/shard_map/all_to_all | solution.py:327
  71.5 0.8 backward_scan.1
  72.3 0.0 copy-done.4
  72.3 12.7 %all-to-all-start.4 = ((bf16[64,8,128]{2,1,0:T(8,128)(2,1)}), bf16[64,8,128]{2,1,0:T(8,128)(2,1)S(1)}, u32[]{:S(2)}, u32[]{:S(2)}) async-start(bf16[64,8,128]{2,1,0:T(8,128)(2,1)} %bitcast.5), calls=%async_computation.4 | async-start | bytes 262144 | tf_op jit(solution)/shard_map/all_to_all | solution.py:327
  85.0 0.0 copy-start.5
  85.0 1.0 %copy-done.5 = bf16[512,512]{1,0:T(8,128)(2,1)S(1)} copy-done((bf16[512,512]{1,0:T(8,128)(2,1)S(1)}, bf16[512,512]{1,0:T(8,128)(2,1)}, u32[]{:S(2)}) %copy-start.5) | copy-done | bytes 524312
  86.1 0.0 copy-start.1
  86.1 0.0 copy-start.2
  86.1 4.8 %local_gradient.1 = (bf16[512,512]{1,0:T(8,128)(2,1)}, bf16[512,512]{1,0:T(8,128)(2,1)S(1)}, bf16[512,512]{1,0:T(8,128)(2,1)S(1)}, f32[1,512]{1,0:T(1,128)}, f32[4,128]{1,0:T(4,128)}) custom-call(bf16[512,512]{1,0:T(8,128)(2,1)S(1)} %copy-done.5, bf16[512,512]{1,0:T(8,128)(2,1)S(1)} %copy-done.3, bf16[512,512]{1,0:T(8,128)(2,1)} %keys.1, ...), custom_call_target="tpu_custom_call" | custom-call | flops 1610612736 | bytes 4345856 | tf_op jit(solution)/shard_map/local_gradient/pallas_call | solution.py:308
  90.8 0.0 all-to-all-done.4
  90.8 0.0 copy-done.1
  90.9 0.0 copy-done.2
  90.9 1.3 %final.1 = (bf16[512,512]{1,0:T(8,128)(2,1)}, bf16[512,512]{1,0:T(8,128)(2,1)}) custom-call(bf16[512,128]{1,0:T(8,128)(2,1)S(1)} %bitcast.10, bf16[512,512]{1,0:T(8,128)(2,1)S(1)} %copy-done.1, bf16[512,512]{1,0:T(8,128)(2,1)S(1)} %copy-done.2, bf16[512,512]{1,0:T(8,128)(2,1)S(1)} %get-tuple-element.44.local_k, ...), custom_call_target="tpu_custom_call" | custom-call | flops 134217728 | bytes 3538944 | tf_op jit(solution)/shard_map/final/pallas_call | solution.py:308
Async XLA Ops:
  0.6 25.8 %copy-start = (bf16[512,512]{1,0:T(8,128)(2,1)S(1)}, bf16[512,512]{1,0:T(8,128)(2,1)}, u32[]{:S(2)}) copy-start(bf16[512,512]{1,0:T(8,128)(2,1)} %target.5) | copy-start | bytes 1572868
  0.6 25.8 %copy-start.3 = (bf16[512,512]{1,0:T(8,128)(2,1)S(1)}, bf16[512,512]{1,0:T(8,128)(2,1)}, u32[]{:S(2)}) copy-start(bf16[512,512]{1,0:T(8,128)(2,1)} %queries.5) | copy-start | bytes 1572868
  54.6 17.8 %copy-start.4 = (bf16[512,512]{1,0:T(8,128)(2,1)}, bf16[512,512]{1,0:T(8,128)(2,1)S(1)}, u32[]{:S(2)}) copy-start(bf16[512,512]{1,0:T(8,128)(2,1)S(1)} %get-tuple-element.40.grad_out) | copy-start | bytes 1572868
  72.3 18.5 %all-to-all-start.4 = ((bf16[64,8,128]{2,1,0:T(8,128)(2,1)}), bf16[64,8,128]{2,1,0:T(8,128)(2,1)S(1)}, u32[]{:S(2)}, u32[]{:S(2)}) async-start(bf16[64,8,128]{2,1,0:T(8,128)(2,1)} %bitcast.5), calls=%async_computation.4 | async-start | bytes 262144 | tf_op jit(solution)/shard_map/all_to_all | solution.py:327
  85.0 1.0 %copy-start.5 = (bf16[512,512]{1,0:T(8,128)(2,1)S(1)}, bf16[512,512]{1,0:T(8,128)(2,1)}, u32[]{:S(2)}) copy-start(bf16[512,512]{1,0:T(8,128)(2,1)} %copy-done.4) | copy-start | bytes 1572868
  86.1 4.8 %copy-start.1 = (bf16[512,512]{1,0:T(8,128)(2,1)S(1)}, bf16[512,512]{1,0:T(8,128)(2,1)}, u32[]{:S(2)}) copy-start(bf16[512,512]{1,0:T(8,128)(2,1)} %keys.1) | copy-start | bytes 1572868
  86.1 4.8 %copy-start.2 = (bf16[512,512]{1,0:T(8,128)(2,1)S(1)}, bf16[512,512]{1,0:T(8,128)(2,1)}, u32[]{:S(2)}) copy-start(bf16[512,512]{1,0:T(8,128)(2,1)} %values.1) | copy-start | bytes 1572868

commit v7 on v6

--- a/solution.py
+++ b/solution.py
@@ -133,7 +133,7 @@
         out[at : at + 16] = jnp.concatenate(both, axis=0).astype(BF16)
 
 
-def backward_scan_kernel(arrived, decays, out):
+def backward_scan_kernel(arrived, decays, mark, out):
     state = jnp.zeros((8, HEAD_DIM), F32)
     for pair in reversed(range(BLOCKS // 2)):
         both = []
@@ -225,7 +225,9 @@
     return [wide[:, head(i)] for i in range(len(rows))]
 
 
-def gradient_kernel(sums, attn, target, gain, weight, turned, out, grad_out):
+def gradient_kernel(
+    sums, attn, target, gain, weight, turned, out_far, grad_out, out, sems
+):
     four = jnp.sum(sums[...], axis=0)
     mean_square = four[0:1] / HIDDEN_DIMENSION + EPS
     inverse = 1.0 / jnp.sqrt(mean_square)
@@ -245,13 +247,18 @@
         grad_out[:, head(h)] = d
         backs.append(mm(turned[head(h), :], d))
     tile = jnp.concatenate(gains, axis=0)
-    for h in range(HEADS):
-        out[h * PER_HEAD : (h + 1) * PER_HEAD] = message(backs[h], tile)
+    moving = []
+    for h in range(HEADS):
+        owners = slice(h * PER_HEAD, (h + 1) * PER_HEAD)
+        out[owners] = message(backs[h], tile)
+        moving.append(copy(out.at[owners], out_far.at[owners], sems.at[h]))
+    for one in moving:
+        one.wait()
 
 
 def local_gradient_kernel(
-    grad_out, queries, keys_far, values_far, states, cum, columns, sums, arrived,
-    grad_q, local_k, local_v, payoff, gain_out, keys, values, sems,
+    grad_out, queries, keys_far, values_far, states, cum, columns, sums,
+    grad_q, local_k, local_v, payoff, mark, keys, values, sems,
 ):
     got_keys = copy(keys_far, keys, sems.at[0])
     got_values = copy(values_far, values, sems.at[1])
@@ -261,10 +268,7 @@
     pred_square = four[1:2] / mean_square
     pred_cross = four[2:3] / jnp.sqrt(mean_square)
     payoff[...] = (pred_square - 2.0 * pred_cross + four[3:4]) / HIDDEN_DIMENSION
-    gains = jnp.zeros((HEADS, HEAD_DIM), F32)
-    for b in range(BLOCKS):
-        gains = gains + received(arrived, b)[1]
-    gain_out[...] = gains / (BLOCKS * TOK)
+    mark[...] = jnp.zeros((8, HEAD_DIM), F32)
     got_keys.wait()
     got_values.wait()
     for h in range(HEADS):
@@ -281,9 +285,14 @@
 
 
 def final_kernel(
-    states, keys, values, local_k, local_v, columns, grad_k_far, grad_v_far, grad_k, grad_v, sems
+    states, keys, values, local_k, local_v, columns, arrived,
+    grad_k_far, grad_v_far, gain_far, grad_k, grad_v, gain, sems,
 ):
-    moving = []
+    gains = jnp.zeros((HEADS, HEAD_DIM), F32)
+    for b in range(BLOCKS):
+        gains = gains + received(arrived, b)[1]
+    gain[...] = gains / (BLOCKS * TOK)
+    moving = [copy(gain, gain_far, sems.at[0])]
     for h in range(HEADS):
         tail, state = columns[:, 16 + h : 17 + h], states[head(h), :]
         for near, far, local, side, dims in (
@@ -366,28 +375,35 @@
     )
     sums = exchange(sums, "head")
     sent, grad_out = call(
-        gradient_kernel, [slices, full16], [sums, attn, target, gain, weight, turned], narrow, "gradient"
+        gradient_kernel,
+        [slices, full16],
+        [sums, attn, target, gain, weight, turned],
+        narrow,
+        "gradient",
+        far_outs=(0,),
+        scratch=[pltpu.VMEM(slices.shape, BF16), pltpu.SemaphoreType.DMA((HEADS,))],
     )
     arrived_back = exchange(sent, "ctx")
-    grad_q, local_k, local_v, payoff, gain_out = call(
+    grad_q, local_k, local_v, payoff, mark = call(
         local_gradient_kernel,
-        [full16, full16, full16, row, shape((HEADS, HEAD_DIM), F32)],
-        [grad_out, queries, keys, values, states, cum, columns, sums, arrived_back],
+        [full16, full16, full16, row, shape((8, HEAD_DIM), F32)],
+        [grad_out, queries, keys, values, states, cum, columns, sums],
         6 * wide,
         "local_gradient",
         far=(2, 3),
         scratch=pair,
     )
-    [later] = call(backward_scan_kernel, [back], [arrived_back, arrived], 1000, "backward_scan")
+    [later] = call(backward_scan_kernel, [back], [arrived_back, arrived, mark], 1000, "backward_scan")
     later = exchange(later.reshape(BLOCKS, 8, HEAD_DIM), "ctx").reshape(TOK, HEAD_DIM)
-    grad_k, grad_v = call(
+    grad_k, grad_v, gain_out = call(
         final_kernel,
-        [full16, full16],
-        [later, keys, values, local_k, local_v, columns],
+        [full16, full16, shape((HEADS, HEAD_DIM), F32)],
+        [later, keys, values, local_k, local_v, columns, arrived_back],
         2 * narrow,
         "final",
-        far_outs=(0, 1),
-        scratch=pair[:2] + [pltpu.SemaphoreType.DMA((2 * HEADS,))],
+        far_outs=(0, 1, 2),
+        scratch=pair[:2]
+        + [pltpu.VMEM((HEADS, HEAD_DIM), F32), pltpu.SemaphoreType.DMA((2 * HEADS + 1,))],
     )
     return payoff.reshape(-1), grad_q, grad_k, grad_v, gain_out.reshape(-1)
 

time: 92.6 us -> 90.5 us (0.977)
  blocking collectives: 66.1 us -> 64.4 us
  local copies, waits for them, and re-layouts: 1.06 us -> 0.02 us
    all_to_all x4, blocking collectives: 66.1 us -> 64.4 us  [exchange(): return lax.all_to_all(x, axis, 0, 0, tiled=True, axis_index_groups=[order])]
    unnamed x12 -> x8, local copies, waits for them, and re-layouts: 1.06 us -> 0.02 us
where the time goes in v7:
time: 90.5 us; the launch traced here: 89.8 us
  blocking collectives  64.4 us (71%)
  starting transfers between devices  13.1 us (14%)
  Pallas kernels  11.6 us (13%)
    all_to_all x4, blocking collectives, exchange(): return lax.all_to_all(x, axis, 0, 0, tiled=True, axis_index_groups=[order])  64.4 us
    all_to_all x1, starting transfers between devices, exchange(): return lax.all_to_all(x, axis, 0, 0, tiled=True, axis_index_groups=[order])  13.1 us
    pallas_call x7, Pallas kernels, call(): pl.pallas_call(kernel, out_shape=outs, in_specs=[FAR_AWAY if i in far els...  11.6 us
  transfers between devices with their start and end apart: 1, of which 0 were waited for; matrix products, arithmetic and copies ran while one was open for 0% of the time, Pallas kernels for 5%

profile of v7, /device:TPU:1, one launch (start us, length us, event | category | flops | bytes accessed | tf_op | source)
XLA Modules:
  0.0 89.8 jit_solution(5566586868321111333)
XLA Ops:
  0.6 0.0 copy-start
  0.6 0.0 copy-start.1
  0.7 1.8 %summary.1 = (bf16[64,4,384]{2,1,0:T(4,128)(2,1)S(1)}, f32[8,512]{1,0:T(8,128)S(1)}, bf16[512,512]{1,0:T(8,128)(2,1)S(1)}, bf16[512,512]{1,0:T(8,128)(2,1)S(1)},...) custom-call(f32[4,512]{1,0:T(4,128)} %retention_far.1, bf16[512,512]{1,0:T(8,128)(2,1)} %keys.1, bf16[512,512]{1,0:T(8,128)(2,1)} %values.1, ...), custom_call_target="tpu_custom_call" | custom-call | flops 67108864 | bytes 2326528 | tf_op jit(solution)/shard_map/summary/pallas_call | solution.py:317
  2.4 24.0 %all_to_all.25.arrived.decays = bf16[64,4,384]{2,1,0:T(4,128)(2,1)S(1)} all-to-all(bf16[64,4,384]{2,1,0:T(4,128)(2,1)S(1)} %get-tuple-element.28), channel_id=1, replica_groups={{288,296,304,312,320,328,336,344,352,360,368,376,384,392,400,408,416,42..., dimensions={0} | all-to-all | bytes 393216 | tf_op jit(solution)/shard_map/all_to_all | solution.py:336
  26.4 0.0 copy-done
  26.4 0.0 copy-done.1
  26.4 1.2 %local.1 = (bf16[512,128]{1,0:T(8,128)(2,1)S(1)}, f32[512,512]{1,0:T(8,128)S(1)}, bf16[512,512]{1,0:T(8,128)(2,1)S(1)}, f32[512,128]{1,0:T(8,128)S(1)}, f32[1,512]{1,0:T(1,128)S(1)}) custom-call(bf16[64,4,384]{2,1,0:T(4,128)(2,1)S(1)} %all_to_all.25.arrived.decays, bf16[512,512]{1,0:T(8,128)(2,1)S(1)} %copy-done.1, ...), custom_call_target="tpu_custom_call" | custom-call | flops 536870912 | bytes 4278272 | tf_op jit(solution)/shard_map/local/pallas_call | solution.py:317
  27.6 15.9 %all_to_all.26 = bf16[64,8,128]{2,1,0:T(8,128)(2,1)S(1)} all-to-all(bf16[64,8,128]{2,1,0:T(8,128)(2,1)S(1)} %bitcast.12), channel_id=1, replica_groups={{288,296,304,312,320,328,336,344,352,360,368,376,384,392,400,408,416,42..., dimensions={0} | all-to-all | bytes 262144 | tf_op jit(solution)/shard_map/all_to_all | solution.py:336
  43.5 0.8 output.1
  44.3 9.3 %all_to_all.27.sums = f32[8,4,512]{2,1,0:T(4,128)S(1)} all-to-all(f32[8,4,512]{2,1,0:T(4,128)S(1)} %get-tuple-element.37), channel_id=1, replica_groups={{4,5,6,7,0,1,2,3},{12,13,14,15,8,9,10,11},{20,21,22,23,16,17,18,19},{28..., dimensions={0} | all-to-all | bytes 131072 | tf_op jit(solution)/shard_map/all_to_all | solution.py:336
  53.6 1.6 %gradient.1 = (bf16[64,4,384]{2,1,0:T(4,128)(2,1)}, bf16[512,512]{1,0:T(8,128)(2,1)S(1)}) custom-call(f32[8,4,512]{2,1,0:T(4,128)S(1)} %all_to_all.27.sums, f32[512,512]{1,0:T(8,128)S(1)} %get-tuple-element.38.attn, bf16[512,512]{1,0:T(8,128)(2,1)S(1)} %copy-done, f32[1,512]{1,0:T(1,128)S(1)} %get-tuple-element.35.gain, ...), custom_call_target="tpu_custom_call" | custom-call | flops 67108864 | bytes 2887680 | tf_op jit(solution)/shard_map/gradient/pallas_call | solution.py:317
  55.2 13.1 %all-to-all-start.3 = ((bf16[64,4,384]{2,1,0:T(4,128)(2,1)}), bf16[64,4,384]{2,1,0:T(4,128)(2,1)S(1)}, u32[]{:S(2)}, u32[]{:S(2)}) async-start(bf16[64,4,384]{2,1,0:T(4,128)(2,1)} %get-tuple-element.44), calls=%async_computation.3 | async-start | bytes 393216 | tf_op jit(solution)/shard_map/all_to_all | solution.py:336
  68.3 0.0 copy-start.3
  68.3 4.8 %local_gradient.1 = (bf16[512,512]{1,0:T(8,128)(2,1)}, bf16[512,512]{1,0:T(8,128)(2,1)S(1)}, bf16[512,512]{1,0:T(8,128)(2,1)S(1)}, f32[1,512]{1,0:T(1,128)}, f32[8,128]{1,0:T(8,128)S(1)}) custom-call(bf16[512,512]{1,0:T(8,128)(2,1)S(1)} %get-tuple-element.41.grad_out, bf16[512,512]{1,0:T(8,128)(2,1)S(1)} %copy-done.1, bf16[512,512]{1,0:T(8,128)(2,1)} %keys.1, ...), custom_call_target="tpu_custom_call" | custom-call | flops 1610612736 | bytes 4151296 | tf_op jit(solution)/shard_map/local_gradient/pallas_call | solution.py:317
  73.1 0.0 copy-start.2
  73.1 0.0 all-to-all-done.3.arrived
  73.1 0.1 backward_scan.1
  73.2 15.2 %all_to_all.28 = bf16[64,8,128]{2,1,0:T(8,128)(2,1)S(1)} all-to-all(bf16[64,8,128]{2,1,0:T(8,128)(2,1)S(1)} %bitcast.10), channel_id=1, replica_groups={{288,296,304,312,320,328,336,344,352,360,368,376,384,392,400,408,416,42..., dimensions={0} | all-to-all | bytes 262144 | tf_op jit(solution)/shard_map/all_to_all | solution.py:336
  88.4 0.0 copy-done.3
  88.4 0.0 copy-done.2
  88.4 1.3 %final.1 = (bf16[512,512]{1,0:T(8,128)(2,1)}, bf16[512,512]{1,0:T(8,128)(2,1)}, f32[4,128]{1,0:T(4,128)}) custom-call(bf16[512,128]{1,0:T(8,128)(2,1)S(1)} %bitcast.11, bf16[512,512]{1,0:T(8,128)(2,1)S(1)} %copy-done.2, bf16[512,512]{1,0:T(8,128)(2,1)S(1)} %copy-done.3, bf16[512,512]{1,0:T(8,128)(2,1)S(1)} %get-tuple-element.46.local_k, ...), custom_call_target="tpu_custom_call" | custom-call | flops 134217728 | bytes 3737600 | tf_op jit(solution)/shard_map/final/pallas_call | solution.py:317
Async XLA Ops:
  0.6 25.8 %copy-start = (bf16[512,512]{1,0:T(8,128)(2,1)S(1)}, bf16[512,512]{1,0:T(8,128)(2,1)}, u32[]{:S(2)}) copy-start(bf16[512,512]{1,0:T(8,128)(2,1)} %target.5) | copy-start | bytes 1572868
  0.6 25.8 %copy-start.1 = (bf16[512,512]{1,0:T(8,128)(2,1)S(1)}, bf16[512,512]{1,0:T(8,128)(2,1)}, u32[]{:S(2)}) copy-start(bf16[512,512]{1,0:T(8,128)(2,1)} %queries.5) | copy-start | bytes 1572868
  55.2 17.9 %all-to-all-start.3 = ((bf16[64,4,384]{2,1,0:T(4,128)(2,1)}), bf16[64,4,384]{2,1,0:T(4,128)(2,1)S(1)}, u32[]{:S(2)}, u32[]{:S(2)}) async-start(bf16[64,4,384]{2,1,0:T(4,128)(2,1)} %get-tuple-element.44), calls=%async_computation.3 | async-start | bytes 393216 | tf_op jit(solution)/shard_map/all_to_all | solution.py:336
  68.3 20.2 %copy-start.3 = (bf16[512,512]{1,0:T(8,128)(2,1)S(1)}, bf16[512,512]{1,0:T(8,128)(2,1)}, u32[]{:S(2)}) copy-start(bf16[512,512]{1,0:T(8,128)(2,1)} %values.1) | copy-start | bytes 1572868
  73.1 15.4 %copy-start.2 = (bf16[512,512]{1,0:T(8,128)(2,1)S(1)}, bf16[512,512]{1,0:T(8,128)(2,1)}, u32[]{:S(2)}) copy-start(bf16[512,512]{1,0:T(8,128)(2,1)} %keys.1) | copy-start | bytes 1572868

commit v8 on v7

--- a/solution.py
+++ b/solution.py
@@ -257,11 +257,10 @@
 
 
 def local_gradient_kernel(
-    grad_out, queries, keys_far, values_far, states, cum, columns, sums,
-    grad_q, local_k, local_v, payoff, mark, keys, values, sems,
+    grad_out, queries, keys, values_far, states, cum, columns, sums,
+    grad_q, local_k, local_v, payoff, mark, values, sem,
 ):
-    got_keys = copy(keys_far, keys, sems.at[0])
-    got_values = copy(values_far, values, sems.at[1])
+    got_values = copy(values_far, values, sem)
     logs = cum[...] * LOG2E
     four = jnp.sum(sums[...], axis=0)
     mean_square = four[0:1] / HIDDEN_DIMENSION + EPS
@@ -269,17 +268,19 @@
     pred_cross = four[2:3] / jnp.sqrt(mean_square)
     payoff[...] = (pred_square - 2.0 * pred_cross + four[3:4]) / HIDDEN_DIMENSION
     mark[...] = jnp.zeros((8, HEAD_DIM), F32)
-    got_keys.wait()
+    decays, probs = [], []
+    for h in range(HEADS):
+        decays.append([block_decay(logs, columns, h, *tile) for tile in TILES])
+        scores = products(queries[:, head(h)], keys[:, head(h)])
+        probs.append([(a * decay).astype(BF16) for a, decay in zip(scores, decays[h])])
     got_values.wait()
     for h in range(HEADS):
         q, k, v, d = queries[:, head(h)], keys[:, head(h)], values[:, head(h)], grad_out[:, head(h)]
         carried = columns[:, 8 + h : 9 + h] * mm(d, states[head(h), :], NT)
-        decays = [block_decay(logs, columns, h, *tile) for tile in TILES]
-        probs = [(a * decay).astype(BF16) for a, decay in zip(products(q, k), decays)]
-        grads = [(a * decay).astype(BF16) for a, decay in zip(products(d, v), decays)]
+        grads = [(a * decay).astype(BF16) for a, decay in zip(products(d, v), decays[h])]
         for rows, part in zip(HALVES, along_rows(grads, k)):
             grad_q[rows, head(h)] = (part + carried[rows]).astype(BF16)
-        for side, tiles, far in ((local_k, grads, q), (local_v, probs, d)):
+        for side, tiles, far in ((local_k, grads, q), (local_v, probs[h], d)):
             for rows, part in zip(HALVES, along_columns(tiles, far)):
                 side[rows, head(h)] = part.astype(BF16)
 
@@ -390,8 +391,8 @@
         [grad_out, queries, keys, values, states, cum, columns, sums],
         6 * wide,
         "local_gradient",
-        far=(2, 3),
-        scratch=pair,
+        far=(3,),
+        scratch=[pltpu.VMEM((TOK, TOK), BF16), pltpu.SemaphoreType.DMA],
     )
     [later] = call(backward_scan_kernel, [back], [arrived_back, arrived, mark], 1000, "backward_scan")
     later = exchange(later.reshape(BLOCKS, 8, HEAD_DIM), "ctx").reshape(TOK, HEAD_DIM)

time: 90.5 us -> 90.6 us (level)
  transfers between devices with their start and end apart: 1 -> 1, of which waited for: 0 -> 1; matrix products, arithmetic and copies ran while one was open for 0% -> 0% of each run, Pallas kernels for 5% -> 5%
where the time goes in v8:
time: 90.6 us; the launch traced here: 89.8 us
  blocking collectives  64.4 us (71%)
  starting transfers between devices  13.1 us (14%)
  Pallas kernels  11.1 us (12%)
    all_to_all x4, blocking collectives, exchange(): return lax.all_to_all(x, axis, 0, 0, tiled=True, axis_index_groups=[order])  64.4 us
    all_to_all x1, starting transfers between devices, exchange(): return lax.all_to_all(x, axis, 0, 0, tiled=True, axis_index_groups=[order])  13.1 us
    pallas_call x7, Pallas kernels, call(): pl.pallas_call(kernel, out_shape=outs, in_specs=[FAR_AWAY if i in far els...  11.1 us
  transfers between devices with their start and end apart: 1, of which 1 were waited for; matrix products, arithmetic and copies ran while one was open for 0% of the time, Pallas kernels for 5%

profile of v8, /device:TPU:1, one launch (start us, length us, event | category | flops | bytes accessed | tf_op | source)
XLA Modules:
  0.0 89.8 jit_solution(1291885611071694923)
XLA Ops:
  0.6 0.0 copy-start
  0.6 0.0 copy-start.1
  0.7 1.8 %summary.1 = (bf16[64,4,384]{2,1,0:T(4,128)(2,1)S(1)}, f32[8,512]{1,0:T(8,128)S(1)}, bf16[512,512]{1,0:T(8,128)(2,1)S(1)}, bf16[512,512]{1,0:T(8,128)(2,1)S(1)},...) custom-call(f32[4,512]{1,0:T(4,128)} %retention_far.1, bf16[512,512]{1,0:T(8,128)(2,1)} %keys.3, bf16[512,512]{1,0:T(8,128)(2,1)} %values.1, ...), custom_call_target="tpu_custom_call" | custom-call | flops 67108864 | bytes 2326528 | tf_op jit(solution)/shard_map/summary/pallas_call | solution.py:318
  2.4 24.0 %all_to_all.25.arrived.decays = bf16[64,4,384]{2,1,0:T(4,128)(2,1)S(1)} all-to-all(bf16[64,4,384]{2,1,0:T(4,128)(2,1)S(1)} %get-tuple-element.28), channel_id=1, replica_groups={{288,296,304,312,320,328,336,344,352,360,368,376,384,392,400,408,416,42..., dimensions={0} | all-to-all | bytes 393216 | tf_op jit(solution)/shard_map/all_to_all | solution.py:337
  26.4 0.0 copy-done
  26.4 0.0 copy-done.1
  26.4 1.2 %local.1 = (bf16[512,128]{1,0:T(8,128)(2,1)S(1)}, f32[512,512]{1,0:T(8,128)S(1)}, bf16[512,512]{1,0:T(8,128)(2,1)S(1)}, f32[512,128]{1,0:T(8,128)S(1)}, f32[1,512]{1,0:T(1,128)S(1)}) custom-call(bf16[64,4,384]{2,1,0:T(4,128)(2,1)S(1)} %all_to_all.25.arrived.decays, bf16[512,512]{1,0:T(8,128)(2,1)S(1)} %copy-done.1, ...), custom_call_target="tpu_custom_call" | custom-call | flops 536870912 | bytes 4278272 | tf_op jit(solution)/shard_map/local/pallas_call | solution.py:318
  27.6 15.9 %all_to_all.26 = bf16[64,8,128]{2,1,0:T(8,128)(2,1)S(1)} all-to-all(bf16[64,8,128]{2,1,0:T(8,128)(2,1)S(1)} %bitcast.12), channel_id=1, replica_groups={{288,296,304,312,320,328,336,344,352,360,368,376,384,392,400,408,416,42..., dimensions={0} | all-to-all | bytes 262144 | tf_op jit(solution)/shard_map/all_to_all | solution.py:337
  43.5 0.8 output.1
  44.3 9.3 %all_to_all.27.sums = f32[8,4,512]{2,1,0:T(4,128)S(1)} all-to-all(f32[8,4,512]{2,1,0:T(4,128)S(1)} %get-tuple-element.37), channel_id=1, replica_groups={{4,5,6,7,0,1,2,3},{12,13,14,15,8,9,10,11},{20,21,22,23,16,17,18,19},{28..., dimensions={0} | all-to-all | bytes 131072 | tf_op jit(solution)/shard_map/all_to_all | solution.py:337
  53.6 0.0 copy-start.2
  53.6 1.6 %gradient.1 = (bf16[64,4,384]{2,1,0:T(4,128)(2,1)}, bf16[512,512]{1,0:T(8,128)(2,1)S(1)}) custom-call(f32[8,4,512]{2,1,0:T(4,128)S(1)} %all_to_all.27.sums, f32[512,512]{1,0:T(8,128)S(1)} %get-tuple-element.38.attn, bf16[512,512]{1,0:T(8,128)(2,1)S(1)} %copy-done, f32[1,512]{1,0:T(1,128)S(1)} %get-tuple-element.35.gain, ...), custom_call_target="tpu_custom_call" | custom-call | flops 67108864 | bytes 2887680 | tf_op jit(solution)/shard_map/gradient/pallas_call | solution.py:318
  55.2 13.1 %all-to-all-start.3 = ((bf16[64,4,384]{2,1,0:T(4,128)(2,1)}), bf16[64,4,384]{2,1,0:T(4,128)(2,1)S(1)}, u32[]{:S(2)}, u32[]{:S(2)}) async-start(bf16[64,4,384]{2,1,0:T(4,128)(2,1)} %get-tuple-element.44), calls=%async_computation.3 | async-start | bytes 393216 | tf_op jit(solution)/shard_map/all_to_all | solution.py:337
  68.3 0.0 copy-done.2
  68.3 4.3 %local_gradient.1 = (bf16[512,512]{1,0:T(8,128)(2,1)}, bf16[512,512]{1,0:T(8,128)(2,1)S(1)}, bf16[512,512]{1,0:T(8,128)(2,1)S(1)}, f32[1,512]{1,0:T(1,128)}, f32[8,128]{1,0:T(8,128)S(1)}) custom-call(bf16[512,512]{1,0:T(8,128)(2,1)S(1)} %get-tuple-element.41.grad_out, bf16[512,512]{1,0:T(8,128)(2,1)S(1)} %copy-done.1, bf16[512,512]{1,0:T(8,128)(2,1)S(1)} %copy-done.2, ...), custom_call_target="tpu_custom_call" | custom-call | flops 1610612736 | bytes 4151296 | tf_op jit(solution)/shard_map/local_gradient/pallas_call | solution.py:318
  72.6 0.0 copy-start.3
  72.6 0.5 all-to-all-done.3.arrived
  73.1 0.1 backward_scan.1
  73.2 15.3 %all_to_all.28 = bf16[64,8,128]{2,1,0:T(8,128)(2,1)S(1)} all-to-all(bf16[64,8,128]{2,1,0:T(8,128)(2,1)S(1)} %bitcast.10), channel_id=1, replica_groups={{288,296,304,312,320,328,336,344,352,360,368,376,384,392,400,408,416,42..., dimensions={0} | all-to-all | bytes 262144 | tf_op jit(solution)/shard_map/all_to_all | solution.py:337
  88.5 0.0 copy-done.3
  88.5 1.3 %final.1 = (bf16[512,512]{1,0:T(8,128)(2,1)}, bf16[512,512]{1,0:T(8,128)(2,1)}, f32[4,128]{1,0:T(4,128)}) custom-call(bf16[512,128]{1,0:T(8,128)(2,1)S(1)} %bitcast.11, bf16[512,512]{1,0:T(8,128)(2,1)S(1)} %copy-done.2, bf16[512,512]{1,0:T(8,128)(2,1)S(1)} %copy-done.3, bf16[512,512]{1,0:T(8,128)(2,1)S(1)} %get-tuple-element.46.local_k, ...), custom_call_target="tpu_custom_call" | custom-call | flops 134217728 | bytes 3737600 | tf_op jit(solution)/shard_map/final/pallas_call | solution.py:318
Async XLA Ops:
  0.6 25.8 %copy-start = (bf16[512,512]{1,0:T(8,128)(2,1)S(1)}, bf16[512,512]{1,0:T(8,128)(2,1)}, u32[]{:S(2)}) copy-start(bf16[512,512]{1,0:T(8,128)(2,1)} %target.5) | copy-start | bytes 1572868
  0.6 25.8 %copy-start.1 = (bf16[512,512]{1,0:T(8,128)(2,1)S(1)}, bf16[512,512]{1,0:T(8,128)(2,1)}, u32[]{:S(2)}) copy-start(bf16[512,512]{1,0:T(8,128)(2,1)} %queries.5) | copy-start | bytes 1572868
  53.6 14.6 %copy-start.2 = (bf16[512,512]{1,0:T(8,128)(2,1)S(1)}, bf16[512,512]{1,0:T(8,128)(2,1)}, u32[]{:S(2)}) copy-start(bf16[512,512]{1,0:T(8,128)(2,1)} %keys.3) | copy-start | bytes 1572868
  55.2 17.8 %all-to-all-start.3 = ((bf16[64,4,384]{2,1,0:T(4,128)(2,1)}), bf16[64,4,384]{2,1,0:T(4,128)(2,1)S(1)}, u32[]{:S(2)}, u32[]{:S(2)}) async-start(bf16[64,4,384]{2,1,0:T(4,128)(2,1)} %get-tuple-element.44), calls=%async_computation.3 | async-start | bytes 393216 | tf_op jit(solution)/shard_map/all_to_all | solution.py:337
  72.6 15.9 %copy-start.3 = (bf16[512,512]{1,0:T(8,128)(2,1)S(1)}, bf16[512,512]{1,0:T(8,128)(2,1)}, u32[]{:S(2)}) copy-start(bf16[512,512]{1,0:T(8,128)(2,1)} %values.1) | copy-start | bytes 1572868
